TPU v7x, 256 devices: a whole 4x4x8 slice. The times are simulated.
256 devices in a mesh: slab: 8 (over z_hi, core), px: 4 (over y), py: 8 (over z_lo, x).
Axes of the slice: x: 4, y: 4, z: 8 (z_hi: 4, z_lo: 2; z = z_hi * 2 + z_lo), core: 2. Of those that a mesh axis runs over, the one named last changes fastest.
Arguments:
- feat: bfloat16 [32, 8, 64, 1024], P(None, 'px', 'py', 'slab'), may hold values from -6 to 6
- w_enc: bfloat16 [32, 32, 3, 3, 3], replicated, may hold values from -0.21875 to 0.21875
- w_down: bfloat16 [64, 32, 3, 3, 3], replicated, may hold values from -0.21875 to 0.21875
- w_dec: bfloat16 [32, 96, 3, 3, 3], replicated, may hold values from -0.125 to 0.125
- cotangent: bfloat16 [32, 8, 64, 1024], P(None, 'px', 'py', 'slab'), may hold values from -6 to 6
Outputs:
- result: bfloat16 [32, 8, 64, 1024], P(None, 'px', 'py', 'slab')
- grad_feat: bfloat16 [32, 8, 64, 1024], P(None, 'px', 'py', 'slab')
- grad_enc: float32 [32, 32, 3, 3, 3], replicated
- grad_down: float32 [64, 32, 3, 3, 3], replicated
- grad_dec: float32 [32, 96, 3, 3, 3], replicated
All inputs are finite; a program needn't handle non-finite values.
Results may differ from a plain program's by a relative error of at most 0.013.
Values may be sent and summed in bfloat16 or wider, within the bound.
A program may use at most 64 MiB of HBM per device.

v0:
```python
import math

import jax
import jax.numpy as jnp
from jax import lax
from jax.sharding import PartitionSpec as P


def padded_2(block, sides, width):
    for axis, dim in sides:
        count = lax.axis_size(axis)
        forward = [(i, i + 1) for i in range(count - 1)]
        backward = [(target, source) for source, target in forward]
        low = lax.ppermute(
            lax.slice_in_dim(block, block.shape[dim] - width, None, axis=dim), axis, forward
        )
        high = lax.ppermute(lax.slice_in_dim(block, 0, width, axis=dim), axis, backward)
        block = jnp.concatenate([low, block, high], axis=dim)
    return block


def conv_valid(padded, weight):
    return lax.conv_general_dilated(
        padded[None],
        weight,
        (1, 1, 1),
        "VALID",
        dimension_numbers=("NCDHW", "OIDHW", "NCDHW"),
        preferred_element_type=jnp.float32,
    )[0]


def flipped(weight):
    return jnp.flip(weight, (2, 3, 4)).swapaxes(0, 1)


def weight_grad(grad_out, padded):
    size_x, size_y, size_z = (grad_out.shape[1], grad_out.shape[2], grad_out.shape[3])
    terms = []
    for offset_x in range(3):
        for offset_y in range(3):
            for offset_z in range(3):
                piece = padded[
                    :,
                    offset_x : offset_x + size_x,
                    offset_y : offset_y + size_y,
                    offset_z : offset_z + size_z,
                ]
                terms.append(
                    jnp.einsum("oxyz,ixyz->oi", grad_out, piece, preferred_element_type=jnp.float32)
                )
    stacked = jnp.stack(terms)
    return stacked.reshape(3, 3, 3, stacked.shape[1], stacked.shape[2]).transpose(3, 4, 0, 1, 2)


def pool_cells(field):
    chans, size_x, size_y, size_z = field.shape
    blocks = field.astype(jnp.float32).reshape(
        chans, size_x // 2, 2, size_y // 2, 2, size_z // 2, 2
    )
    return blocks.mean(axis=(2, 4, 6)).astype(jnp.bfloat16)


def fold_cells(field):
    chans, size_x, size_y, size_z = field.shape
    return field.reshape(chans, size_x // 2, 2, size_y // 2, 2, size_z // 2, 2).sum(axis=(2, 4, 6))


def upsample(field):
    return jnp.repeat(jnp.repeat(jnp.repeat(field, 2, 1), 2, 2), 2, 3)


def silu_slope(value):
    sig = jax.nn.sigmoid(value)
    return sig * (1.0 + value * (1.0 - sig))


def pad_second(field):
    return jnp.pad(field, ((0, 0), (0, 0), (1, 1), (0, 0)))


def shards(feat, w_enc, w_down, w_dec, cotangent):
    channels, size_x, size_y, size_z = feat.shape
    coarse_channels = w_down.shape[0]
    coarse_rows = size_y // 2
    feat_pad = padded_2(feat, (("slab", 3), ("px", 1), ("py", 2)), 1)
    enc_pre = conv_valid(feat_pad, w_enc)
    skip = jax.nn.silu(enc_pre).astype(jnp.bfloat16)
    pooled = pool_cells(skip)
    row_start = lax.axis_index("py") * coarse_rows
    pooled_all = lax.all_gather(pooled, "py", axis=2, tiled=True)
    pooled_wide = pad_second(padded_2(pooled_all, (("slab", 3), ("px", 1)), 1))
    down_wide = conv_valid(pooled_wide, w_down)
    down_pre = lax.dynamic_slice_in_dim(down_wide, row_start, coarse_rows, 2)
    coarse = jax.nn.silu(down_pre).astype(jnp.bfloat16)
    joined = jnp.concatenate([upsample(coarse), skip], axis=0)
    joined_pad = padded_2(joined, (("slab", 3), ("px", 1), ("py", 2)), 1)
    result = conv_valid(joined_pad, w_dec).astype(jnp.bfloat16)
    cot_pad = padded_2(cotangent, (("slab", 3), ("px", 1), ("py", 2)), 1)
    grad_joined = conv_valid(cot_pad, flipped(w_dec))
    dec_sum = weight_grad(cotangent, joined_pad)
    grad_coarse = (fold_cells(grad_joined[:coarse_channels]) * silu_slope(down_pre)).astype(
        jnp.bfloat16
    )
    grad_all = lax.all_gather(grad_coarse, "py", axis=2, tiled=True)
    grad_wide = pad_second(padded_2(grad_all, (("slab", 3), ("px", 1)), 1))
    pooled_grad_wide = conv_valid(grad_wide, flipped(w_down))
    grad_pooled = lax.dynamic_slice_in_dim(pooled_grad_wide, row_start, coarse_rows, 2)
    down_sum = weight_grad(grad_all, pooled_wide) * (1.0 / float(lax.axis_size("py")))
    grad_skip = (
        (grad_joined[coarse_channels:] + upsample(grad_pooled) * 0.125) * silu_slope(enc_pre)
    ).astype(jnp.bfloat16)
    enc_sum = weight_grad(grad_skip, feat_pad)
    skip_grad_pad = padded_2(grad_skip, (("slab", 3), ("px", 1), ("py", 2)), 1)
    grad_feat = conv_valid(skip_grad_pad, flipped(w_enc)).astype(jnp.bfloat16)
    enc_sum, down_sum, dec_sum = lax.psum((enc_sum, down_sum, dec_sum), ("slab", "px", "py"))
    total_cells = (
        size_x * size_y * size_z * lax.axis_size("slab") * lax.axis_size("px") * lax.axis_size("py")
    )
    scale = 1.0 / math.sqrt(float(total_cells))
    return (result, grad_feat, enc_sum * scale, down_sum * scale, dec_sum * scale)


def solution(mesh):
    placed = (P(None, "px", "py", "slab"), P(), P(), P(), P(None, "px", "py", "slab"))
    return jax.shard_map(
        shards,
        mesh=mesh,
        in_specs=placed,
        out_specs=(P(None, "px", "py", "slab"), P(None, "px", "py", "slab"), P(), P(), P()),
        check_vma=False,
    )
```

profile of v0, /device:TPU:1, one launch (start us, length us, event | category | flops | bytes accessed | tf_op | source)
XLA Modules:
  0.0 573.4 jit_solution(10930461602581246889)
XLA Ops:
  8.4 5.3 collective-permute-start.17
  19.7 4.5 collective-permute-start
  26.7 4.0 collective-permute-start.18
  32.3 4.0 collective-permute-start.2
  38.0 4.0 collective-permute-start.20
  43.4 4.0 collective-permute-start.4
  62.5 22.8 %all-gather = bf16[32,32,64]{2,0,1:T(8,128)(2,1)S(1)} all-gather(bf16[32,4,64]{2,0,1:T(8,128)(2,1)S(1)} %multiply_convert_fusion.1), channel_id=2, replica_groups=mesh['slab'=8,'px'=4,'py'=8] {'py'}, dimensions={1}, use_global_device_ids=true | all-gather | bytes 147456 | tf_op jit(solution)/shard_map/all_gather | solution.py:91
  86.2 8.5 %collective-permute-start.7 = (bf16[32,1,32,1]{3,0,2,1:T(8,128)(2,1)}, bf16[32,1,32,1]{3,0,2,1:T(8,128)(2,1)S(1)}, u32[]{:S(2)}, u32[]{:S(2)}) collective-permute-start(bf16[32,1,32,1]{3,0,2,1:T(8,128)(2,1)} %get-tuple-element.62), channel_id=1, source_target_pairs={{32,0},{64,32},{96,64},{128,96},{160,128},{192,160},{224,192},{33,... | collective-permute-start | bytes 6152 | tf_op jit(solution)/shard_map/ppermute | solution.py:17
  94.7 5.7 collective-permute-start.6
  110.3 4.0 collective-permute-start.8
  127.1 3.8 fusion.74
  131.5 23.4 %all_gather.7 = bf16[64,1,32,64]{3,0,1,2:T(8,128)(2,1)S(1)} all-gather(bf16[64,1,4,64]{3,0,1,2:T(8,128)(2,1)S(1)} %fusion.279), channel_id=1, replica_groups=mesh['slab'=8,'px'=4,'py'=8] {'py'}, dimensions={2}, use_global_device_ids=true | all-gather | bytes 294912 | tf_op jit(solution)/shard_map/all_gather | solution.py:105
  155.2 5.5 collective-permute-start.23
  160.7 6.9 %collective-permute-start.22 = (bf16[64,1,32,1]{3,0,1,2:T(8,128)(2,1)S(1)}, bf16[64,1,32,1]{3,0,1,2:T(8,128)(2,1)S(1)}, u32[]{:S(2)}, u32[]{:S(2)}) collective-permute-start(bf16[64,1,32,1]{3,0,1,2:T(8,128)(2,1)S(1)} %get-tuple-element.49), channel_id=1, source_target_pairs={{0,32},{32,64},{64,96},{96,128},{128,160},{160,192},{192,224},{1,3... | collective-permute-start | bytes 12296 | tf_op jit(solution)/shard_map/ppermute | solution.py:14
  178.8 13.7 %collective-permute-start.24 = (bf16[64,1,32,66]{3,0,1,2:T(8,128)(2,1)S(1)}, bf16[64,1,32,66]{3,0,1,2:T(8,128)(2,1)}, u32[]{:S(2)}, u32[]{:S(2)}) collective-permute-start(bf16[64,1,32,66]{3,0,1,2:T(8,128)(2,1)S(1)} %pad_maximum_fusion.5), channel_id=1, source_target_pairs={{0,8},{8,16},{16,24},{1,9},{9,17},{17,25},{2,10},{10,18},{18,26},{... | collective-permute-start | bytes 811016 | tf_op jit(solution)/shard_map/ppermute | solution.py:14
  202.3 4.5 fusion.77
  210.6 4.5 collective-permute-start.10
  217.1 5.9 %collective-permute-start.26 = (bf16[32,2,8,1]{3,0,2,1:T(8,128)(2,1)S(1)}, bf16[32,2,8,1]{3,0,2,1:T(8,128)(2,1)S(1)}, u32[]{:S(2)}, u32[]{:S(2)}) collective-permute-start(bf16[32,2,8,1]{3,0,2,1:T(8,128)(2,1)S(1)} %get-tuple-element.65), channel_id=1, source_target_pairs={{0,32},{32,64},{64,96},{96,128},{128,160},{160,192},{192,224},{1,3... | collective-permute-start | bytes 3080 | tf_op jit(solution)/shard_map/ppermute | solution.py:14
  231.3 4.0 collective-permute-start.28
  238.7 6.0 %collective-permute-start.30 = (bf16[32,4,1,130]{3,0,2,1:T(8,128)(2,1)S(1)}, bf16[32,4,1,130]{3,0,2,1:T(8,128)(2,1)S(1)}, u32[]{:S(2)}, u32[]{:S(2)}) collective-permute-start(bf16[32,4,1,130]{3,0,2,1:T(8,128)(2,1)S(1)} %get-tuple-element.43), channel_id=1, source_target_pairs={{0,1},{1,2},{2,3},{3,4},{4,5},{5,6},{6,7},{8,9},{9,10},{10,11},{11... | collective-permute-start | bytes 99848 | tf_op jit(solution)/shard_map/ppermute | solution.py:14
  246.8 4.6 collective-permute-start.12
  261.5 4.0 collective-permute-start.14
  290.4 4.0 fusion.68
  295.6 266.0 %all-reduce.5.cloned.1.call-done = (f32[32,32,3,3,3]{1,0,4,3,2:T(8,128)}, f32[64,32,3,3,3]{0,1,4,3,2:T(8,128)}, f32[32,96,3,3,3]{1,0,4,3,2:T(8,128)}) async-done(((f32[32,32,3,3,3]{1,0,4,3,2:T(8,128)}, f32[64,32,3,3,3]{0,1,4,3,2:T(8,128)}, f32[32,96,3,3,3]{1,0,4,3,2:T(8,128)}), (f32[32,32,3,3,3]{1,0,4,3,2:T(8,128)}, f32[64,32,3,3,3]{0,1,4,3,2:T(8,128)}, ...) | async-done | bytes 663568 | tf_op jit(solution)/shard_map/psum | solution.py:116
  (310 shorter events, 133.9 us)
Async XLA Ops:
  7.2 554.5 %all-reduce.5.cloned.1.call-start = ((), (), s32[]{:S(2)}) async-start(), calls=%async_computation | async-start | bytes 2654208 | tf_op jit(solution)/shard_map/psum | solution.py:116
  8.4 15.9 %collective-permute-start.17 = (bf16[32,2,8,1]{3,2,1,0:T(8,128)(2,1)S(1)}, bf16[32,2,8,1]{3,2,1,0:T(8,128)(2,1)S(1)}, u32[]{:S(2)}, u32[]{:S(2)}) collective-permute-start(bf16[32,2,8,1]{3,2,1,0:T(8,128)(2,1)S(1)} %get-tuple-element.68), channel_id=1, source_target_pairs={{32,0},{64,32},{96,64},{128,96},{160,128},{192,160},{224,192},{33,... | collective-permute-start | bytes 3080 | tf_op jit(solution)/shard_map/ppermute | solution.py:17
  13.7 10.6 %collective-permute-start.16 = (bf16[32,2,8,1]{3,2,1,0:T(8,128)(2,1)S(1)}, bf16[32,2,8,1]{3,2,1,0:T(8,128)(2,1)S(1)}, u32[]{:S(2)}, u32[]{:S(2)}) collective-permute-start(bf16[32,2,8,1]{3,2,1,0:T(8,128)(2,1)S(1)} %get-tuple-element.67), channel_id=1, source_target_pairs={{0,32},{32,64},{64,96},{96,128},{128,160},{160,192},{192,224},{1,3... | collective-permute-start | bytes 3080 | tf_op jit(solution)/shard_map/ppermute | solution.py:14
  17.8 12.9 %collective-permute-start.1 = (bf16[32,2,8,1]{3,0,2,1:T(8,128)(2,1)S(1)}, bf16[32,2,8,1]{3,0,2,1:T(8,128)(2,1)S(1)}, u32[]{:S(2)}, u32[]{:S(2)}) collective-permute-start(bf16[32,2,8,1]{3,0,2,1:T(8,128)(2,1)S(1)} %get-tuple-element.70), channel_id=1, source_target_pairs={{32,0},{64,32},{96,64},{128,96},{160,128},{192,160},{224,192},{33,... | collective-permute-start | bytes 3080 | tf_op jit(solution)/shard_map/ppermute | solution.py:17
  19.7 11.0 %collective-permute-start = (bf16[32,2,8,1]{3,0,2,1:T(8,128)(2,1)S(1)}, bf16[32,2,8,1]{3,0,2,1:T(8,128)(2,1)S(1)}, u32[]{:S(2)}, u32[]{:S(2)}) collective-permute-start(bf16[32,2,8,1]{3,0,2,1:T(8,128)(2,1)S(1)} %get-tuple-element.69), channel_id=1, source_target_pairs={{0,32},{32,64},{64,96},{96,128},{128,160},{160,192},{192,224},{1,3... | collective-permute-start | bytes 3080 | tf_op jit(solution)/shard_map/ppermute | solution.py:14
  25.4 10.9 %collective-permute-start.19 = (bf16[32,1,8,130]{3,2,1,0:T(8,128)(2,1)S(1)}, bf16[32,1,8,130]{3,2,1,0:T(8,128)(2,1)S(1)}, u32[]{:S(2)}, u32[]{:S(2)}) collective-permute-start(bf16[32,1,8,130]{3,2,1,0:T(8,128)(2,1)S(1)} %get-tuple-element.60), channel_id=1, source_target_pairs={{8,0},{16,8},{24,16},{9,1},{17,9},{25,17},{10,2},{18,10},{26,18},{... | collective-permute-start | bytes 199688 | tf_op jit(solution)/shard_map/ppermute | solution.py:17
  31.0 11.0 %collective-permute-start.3 = (bf16[32,1,8,130]{3,0,2,1:T(8,128)(2,1)S(1)}, bf16[32,1,8,130]{3,0,2,1:T(8,128)(2,1)S(1)}, u32[]{:S(2)}, u32[]{:S(2)}) collective-permute-start(bf16[32,1,8,130]{3,0,2,1:T(8,128)(2,1)S(1)} %get-tuple-element.64), channel_id=1, source_target_pairs={{8,0},{16,8},{24,16},{9,1},{17,9},{25,17},{10,2},{18,10},{26,18},{... | collective-permute-start | bytes 199688 | tf_op jit(solution)/shard_map/ppermute | solution.py:17
  36.7 11.9 %collective-permute-start.21 = (bf16[32,4,1,130]{3,2,1,0:T(2,128)(2,1)S(1)}, bf16[32,4,1,130]{3,2,1,0:T(2,128)(2,1)S(1)}, u32[]{:S(2)}, u32[]{:S(2)}) collective-permute-start(bf16[32,4,1,130]{3,2,1,0:T(2,128)(2,1)S(1)} %get-tuple-element.46), channel_id=1, source_target_pairs={{1,0},{2,1},{3,2},{4,3},{5,4},{6,5},{7,6},{9,8},{10,9},{11,10},{12... | collective-permute-start | bytes 99848 | tf_op jit(solution)/shard_map/ppermute | solution.py:17
  38.0 10.6 %collective-permute-start.20 = (bf16[32,4,1,130]{3,2,1,0:T(2,128)(2,1)S(1)}, bf16[32,4,1,130]{3,2,1,0:T(2,128)(2,1)S(1)}, u32[]{:S(2)}, u32[]{:S(2)}) collective-permute-start(bf16[32,4,1,130]{3,2,1,0:T(2,128)(2,1)S(1)} %get-tuple-element.45), channel_id=1, source_target_pairs={{0,1},{1,2},{2,3},{3,4},{4,5},{5,6},{6,7},{8,9},{9,10},{10,11},{11... | collective-permute-start | bytes 99848 | tf_op jit(solution)/shard_map/ppermute | solution.py:14
  42.1 11.5 %collective-permute-start.5 = (bf16[32,4,1,130]{3,0,2,1:T(8,128)(2,1)S(1)}, bf16[32,4,1,130]{3,0,2,1:T(8,128)(2,1)S(1)}, u32[]{:S(2)}, u32[]{:S(2)}) collective-permute-start(bf16[32,4,1,130]{3,0,2,1:T(8,128)(2,1)S(1)} %get-tuple-element.48), channel_id=1, source_target_pairs={{1,0},{2,1},{3,2},{4,3},{5,4},{6,5},{7,6},{9,8},{10,9},{11,10},{12... | collective-permute-start | bytes 99848 | tf_op jit(solution)/shard_map/ppermute | solution.py:17
  86.2 22.5 %collective-permute-start.7 = (bf16[32,1,32,1]{3,0,2,1:T(8,128)(2,1)}, bf16[32,1,32,1]{3,0,2,1:T(8,128)(2,1)S(1)}, u32[]{:S(2)}, u32[]{:S(2)}) collective-permute-start(bf16[32,1,32,1]{3,0,2,1:T(8,128)(2,1)} %get-tuple-element.62), channel_id=1, source_target_pairs={{32,0},{64,32},{96,64},{128,96},{160,128},{192,160},{224,192},{33,... | collective-permute-start | bytes 6152 | tf_op jit(solution)/shard_map/ppermute | solution.py:17
  94.7 14.1 %collective-permute-start.6 = (bf16[32,1,32,1]{3,0,2,1:T(8,128)(2,1)}, bf16[32,1,32,1]{3,0,2,1:T(8,128)(2,1)S(1)}, u32[]{:S(2)}, u32[]{:S(2)}) collective-permute-start(bf16[32,1,32,1]{3,0,2,1:T(8,128)(2,1)} %get-tuple-element.61), channel_id=1, source_target_pairs={{0,32},{32,64},{64,96},{96,128},{128,160},{160,192},{192,224},{1,3... | collective-permute-start | bytes 6152 | tf_op jit(solution)/shard_map/ppermute | solution.py:14
  155.2 21.1 %collective-permute-start.23 = (bf16[64,1,32,1]{3,0,1,2:T(8,128)(2,1)S(1)}, bf16[64,1,32,1]{3,0,1,2:T(8,128)(2,1)S(1)}, u32[]{:S(2)}, u32[]{:S(2)}) collective-permute-start(bf16[64,1,32,1]{3,0,1,2:T(8,128)(2,1)S(1)} %get-tuple-element.50), channel_id=1, source_target_pairs={{32,0},{64,32},{96,64},{128,96},{160,128},{192,160},{224,192},{33,... | collective-permute-start | bytes 12296 | tf_op jit(solution)/shard_map/ppermute | solution.py:17
  160.7 16.4 %collective-permute-start.22 = (bf16[64,1,32,1]{3,0,1,2:T(8,128)(2,1)S(1)}, bf16[64,1,32,1]{3,0,1,2:T(8,128)(2,1)S(1)}, u32[]{:S(2)}, u32[]{:S(2)}) collective-permute-start(bf16[64,1,32,1]{3,0,1,2:T(8,128)(2,1)S(1)} %get-tuple-element.49), channel_id=1, source_target_pairs={{0,32},{32,64},{64,96},{96,128},{128,160},{160,192},{192,224},{1,3... | collective-permute-start | bytes 12296 | tf_op jit(solution)/shard_map/ppermute | solution.py:14
  177.5 17.3 %collective-permute-start.25 = (bf16[64,1,32,66]{3,0,1,2:T(8,128)(2,1)S(1)}, bf16[64,1,32,66]{3,0,1,2:T(8,128)(2,1)}, u32[]{:S(2)}, u32[]{:S(2)}) collective-permute-start(bf16[64,1,32,66]{3,0,1,2:T(8,128)(2,1)S(1)} %pad_maximum_fusion.5), channel_id=1, source_target_pairs={{8,0},{16,8},{24,16},{9,1},{17,9},{25,17},{10,2},{18,10},{26,18},{... | collective-permute-start | bytes 811016 | tf_op jit(solution)/shard_map/ppermute | solution.py:17
  178.8 16.0 %collective-permute-start.24 = (bf16[64,1,32,66]{3,0,1,2:T(8,128)(2,1)S(1)}, bf16[64,1,32,66]{3,0,1,2:T(8,128)(2,1)}, u32[]{:S(2)}, u32[]{:S(2)}) collective-permute-start(bf16[64,1,32,66]{3,0,1,2:T(8,128)(2,1)S(1)} %pad_maximum_fusion.5), channel_id=1, source_target_pairs={{0,8},{8,16},{16,24},{1,9},{9,17},{17,25},{2,10},{10,18},{18,26},{... | collective-permute-start | bytes 811016 | tf_op jit(solution)/shard_map/ppermute | solution.py:14
  208.5 26.8 %collective-permute-start.11 = (bf16[96,2,8,1]{3,0,2,1:T(8,128)(2,1)S(1)}, bf16[96,2,8,1]{3,0,2,1:T(8,128)(2,1)S(1)}, u32[]{:S(2)}, u32[]{:S(2)}) collective-permute-start(bf16[96,2,8,1]{3,0,2,1:T(8,128)(2,1)S(1)} %get-tuple-element.54), channel_id=1, source_target_pairs={{32,0},{64,32},{96,64},{128,96},{160,128},{192,160},{224,192},{33,... | collective-permute-start | bytes 9224 | tf_op jit(solution)/shard_map/ppermute | solution.py:17
  210.6 24.8 %collective-permute-start.10 = (bf16[96,2,8,1]{3,0,2,1:T(8,128)(2,1)S(1)}, bf16[96,2,8,1]{3,0,2,1:T(8,128)(2,1)S(1)}, u32[]{:S(2)}, u32[]{:S(2)}) collective-permute-start(bf16[96,2,8,1]{3,0,2,1:T(8,128)(2,1)S(1)} %get-tuple-element.53), channel_id=1, source_target_pairs={{0,32},{32,64},{64,96},{96,128},{128,160},{160,192},{192,224},{1,3... | collective-permute-start | bytes 9224 | tf_op jit(solution)/shard_map/ppermute | solution.py:14
  215.2 13.8 %collective-permute-start.27 = (bf16[32,2,8,1]{3,0,2,1:T(8,128)(2,1)S(1)}, bf16[32,2,8,1]{3,0,2,1:T(8,128)(2,1)S(1)}, u32[]{:S(2)}, u32[]{:S(2)}) collective-permute-start(bf16[32,2,8,1]{3,0,2,1:T(8,128)(2,1)S(1)} %get-tuple-element.66), channel_id=1, source_target_pairs={{32,0},{64,32},{96,64},{128,96},{160,128},{192,160},{224,192},{33,... | collective-permute-start | bytes 3080 | tf_op jit(solution)/shard_map/ppermute | solution.py:17
  217.1 12.7 %collective-permute-start.26 = (bf16[32,2,8,1]{3,0,2,1:T(8,128)(2,1)S(1)}, bf16[32,2,8,1]{3,0,2,1:T(8,128)(2,1)S(1)}, u32[]{:S(2)}, u32[]{:S(2)}) collective-permute-start(bf16[32,2,8,1]{3,0,2,1:T(8,128)(2,1)S(1)} %get-tuple-element.65), channel_id=1, source_target_pairs={{0,32},{32,64},{64,96},{96,128},{128,160},{160,192},{192,224},{1,3... | collective-permute-start | bytes 3080 | tf_op jit(solution)/shard_map/ppermute | solution.py:14
  237.4 14.1 %collective-permute-start.31 = (bf16[32,4,1,130]{3,0,2,1:T(8,128)(2,1)S(1)}, bf16[32,4,1,130]{3,0,2,1:T(8,128)(2,1)S(1)}, u32[]{:S(2)}, u32[]{:S(2)}) collective-permute-start(bf16[32,4,1,130]{3,0,2,1:T(8,128)(2,1)S(1)} %get-tuple-element.44), channel_id=1, source_target_pairs={{1,0},{2,1},{3,2},{4,3},{5,4},{6,5},{7,6},{9,8},{10,9},{11,10},{12... | collective-permute-start | bytes 99848 | tf_op jit(solution)/shard_map/ppermute | solution.py:17
  238.7 12.8 %collective-permute-start.30 = (bf16[32,4,1,130]{3,0,2,1:T(8,128)(2,1)S(1)}, bf16[32,4,1,130]{3,0,2,1:T(8,128)(2,1)S(1)}, u32[]{:S(2)}, u32[]{:S(2)}) collective-permute-start(bf16[32,4,1,130]{3,0,2,1:T(8,128)(2,1)S(1)} %get-tuple-element.43), channel_id=1, source_target_pairs={{0,1},{1,2},{2,3},{3,4},{4,5},{5,6},{6,7},{8,9},{9,10},{10,11},{11... | collective-permute-start | bytes 99848 | tf_op jit(solution)/shard_map/ppermute | solution.py:14
  245.5 14.5 %collective-permute-start.13 = (bf16[96,1,8,130]{3,0,2,1:T(8,128)(2,1)}, bf16[96,1,8,130]{3,0,2,1:T(8,128)(2,1)S(1)}, u32[]{:S(2)}, u32[]{:S(2)}) collective-permute-start(bf16[96,1,8,130]{3,0,2,1:T(8,128)(2,1)} %get-tuple-element.40), channel_id=1, source_target_pairs={{8,0},{16,8},{24,16},{9,1},{17,9},{25,17},{10,2},{18,10},{26,18},{... | collective-permute-start | bytes 599048 | tf_op jit(solution)/shard_map/ppermute | solution.py:17
  246.8 13.2 %collective-permute-start.12 = (bf16[96,1,8,130]{3,0,2,1:T(8,128)(2,1)S(1)}, bf16[96,1,8,130]{3,0,2,1:T(8,128)(2,1)S(1)}, u32[]{:S(2)}, u32[]{:S(2)}) collective-permute-start(bf16[96,1,8,130]{3,0,2,1:T(8,128)(2,1)S(1)} %get-tuple-element.39), channel_id=1, source_target_pairs={{0,8},{8,16},{16,24},{1,9},{9,17},{17,25},{2,10},{10,18},{18,26},{... | collective-permute-start | bytes 599048 | tf_op jit(solution)/shard_map/ppermute | solution.py:14
  (48 other events, 558.7 us)
Sparse Core Ops, SparseCore 0:
  290.6 271.0 all-reduce.4
where the time goes:
time: 582 us; the launch traced here: 573 us
  waiting for transfers between devices  271 us (47%)
  starting transfers between devices  121 us (21%)
  local copies, waits for them, and re-layouts  49.8 us (9%)
  blocking collectives  46.3 us (8%)
  matrix products  42.5 us (7%)
  other arithmetic  26.8 us (5%)
  between operations  15.8 us (3%)
    psum x1, waiting for transfers between devices, shards(): lax.psum((enc_sum, down_sum, dec_sum), ('slab', 'px', 'py'))  266 us
    ppermute x16, starting transfers between devices, padded_2(): lax.ppermute(lax.slice_in_dim(block, block.shape[dim] - width, None, axis...  82.9 us
    ppermute x16, starting transfers between devices, padded_2(): lax.ppermute(lax.slice_in_dim(block, 0, width, axis=dim), axis, backward)  38 us
    unnamed x91, local copies, waits for them, and re-layouts  29.2 us
    all_gather x1, blocking collectives, shards(): grad_all = lax.all_gather(grad_coarse, 'py', axis=2, tiled=True)  23.4 us
    all_gather x1, blocking collectives, shards(): pooled_all = lax.all_gather(pooled, 'py', axis=2, tiled=True)  22.8 us
    dot_general x81, matrix products, weight_grad(): jnp.einsum('oxyz,ixyz->oi', grad_out, piece, preferred_element_type=jnp.f...  22.4 us
    conv_general_dilated x6, matrix products, conv_valid(): lax.conv_general_dilated(padded[None], weight, (1, 1, 1), 'VALID', dimens...  20.1 us
  transfers between devices with their start and end apart: 33, of which 5 were waited for; matrix products, arithmetic and copies ran while one was open for 9% of the time, Pallas kernels for 0%

commit v1 on v0

v1 whole, which is shorter than its diff:
```python
import functools
import math

import jax
import jax.numpy as jnp
from jax import lax
from jax.experimental import pallas as pl
from jax.experimental.pallas import tpu as pltpu
from jax.sharding import PartitionSpec as P

MESH = pl.DeviceIdType.MESH
BF = jnp.bfloat16
F32 = jnp.float32
L = 128
TAPS = [(kx, ky, kz) for kz in range(3) for ky in range(3) for kx in range(3)]
PLACE = [kx * 9 + ky * 3 + kz for kx, ky, kz in TAPS]
AROUND = [(dx, dy) for dx in (-1, 0, 1) for dy in (-1, 0, 1) if (dx, dy) != (0, 0)]


def dot(a, b):
    return jnp.dot(a, b, preferred_element_type=F32)


def dot_t(a, b):
    return lax.dot_general(a, b, (((1,), (1,)), ((), ())), preferred_element_type=F32)


def lanes():
    return lax.broadcasted_iota(jnp.int32, (1, L), 1)


def pair_sum(value):
    even = lax.rem(lanes(), 2) == 0
    return value + jnp.where(even, pltpu.roll(value, L - 1, 1), pltpu.roll(value, 1, 1))


def silu_slope(value):
    sig = jax.nn.sigmoid(value)
    return sig * (1.0 + value * (1.0 - sig))


class Halo:
    def __init__(self, at, sizes, field, sent, edge, sems, ny, nx, width):
        self.at, self.sizes, self.field, self.sent, self.edge = at, sizes, field, sent, edge
        self.send, self.recv = sems
        self.ny, self.nx, self.width = ny, nx, width

    def has(self, dx, dy):
        _, px, py = self.at
        _, nx, ny = self.sizes
        return (px + dx >= 0) & (px + dx < nx) & (py + dy >= 0) & (py + dy < ny)

    def plane_copy(self, index):
        dx, dy = AROUND[index]

        def spans(step, size):
            source = {-1: pl.ds(1, 1), 0: pl.ds(1, size), 1: pl.ds(size, 1)}[step]
            target = {-1: pl.ds(size + 1, 1), 0: pl.ds(1, size), 1: pl.ds(0, 1)}[step]
            return source, target

        (sx, tx), (sy, ty) = spans(dx, self.nx), spans(dy, self.ny)
        slab, px, py = self.at
        return pltpu.make_async_remote_copy(
            src_ref=self.field.at[sy, sx],
            dst_ref=self.field.at[ty, tx],
            send_sem=self.send.at[index],
            recv_sem=self.recv.at[index],
            device_id=(slab, px + dx, py + dy),
            device_id_type=MESH,
        )

    def start_plane(self):
        for index, (dx, dy) in enumerate(AROUND):
            pl.when(self.has(dx, dy))(lambda index=index: self.plane_copy(index).start())

    def wait_plane(self):
        for index, (dx, dy) in enumerate(AROUND):
            pl.when(self.has(-dx, -dy))(lambda index=index: self.plane_copy(index).wait_recv())

    def depth_copy(self, side):
        slab, px, py = self.at
        return pltpu.make_async_remote_copy(
            src_ref=self.sent.at[side],
            dst_ref=self.edge.at[side],
            send_sem=self.send.at[8 + side],
            recv_sem=self.recv.at[8 + side],
            device_id=(slab + 1 - 2 * side, px, py),
            device_id_type=MESH,
        )

    def depth_has(self, side, sending):
        up = (side == 0) == sending
        return self.at[0] < self.sizes[0] - 1 if up else self.at[0] > 0

    def start_depth(self):
        width, across = self.width, self.nx + 2
        channels = self.field.shape[2]
        place = lanes() // width

        def step(y, held):
            last, first = held
            for x in range(across):
                row = self.field[y, x].astype(F32)
                index = y * across + x
                last = jnp.where(place == index, pltpu.roll(row, lax.rem(width * index + width, L), 1), last)
                first = jnp.where(place == index, pltpu.roll(row, width * index, 1), first)
            return last, first

        zero = jnp.zeros((channels, L), F32)
        last, first = lax.fori_loop(0, self.ny + 2, step, (zero, zero))
        self.sent[0] = last.astype(BF)
        self.sent[1] = first.astype(BF)
        for side in (0, 1):
            pl.when(self.depth_has(side, True))(lambda side=side: self.depth_copy(side).start())

    def wait_depth(self):
        for side in (0, 1):
            pl.when(self.depth_has(side, False))(lambda side=side: self.depth_copy(side).wait_recv())

    def wait_sent(self):
        for index, (dx, dy) in enumerate(AROUND):
            pl.when(self.has(dx, dy))(lambda index=index: self.plane_copy(index).wait_send())
        for side in (0, 1):
            pl.when(self.depth_has(side, True))(lambda side=side: self.depth_copy(side).wait_send())

    def shift(self, span, low, high, by):
        width, across = self.width, self.nx + 2
        lane = lanes()
        left = self.edge[0, span].astype(F32)
        right = self.edge[1, span].astype(F32)

        def step(y, carry):
            for x in range(across):
                row = self.field[y, x, span].astype(F32)
                index = y * across + x
                first = pltpu.roll(left, lax.rem(L - width * index, L), 1)
                last = pltpu.roll(right, L - by - width * index, 1)
                low[y, x] = jnp.where(lane < by, first, pltpu.roll(row, by, 1)).astype(BF)
                high[y, x] = jnp.where(lane >= L - by, last, pltpu.roll(row, L - by, 1)).astype(BF)
            return carry

        lax.fori_loop(0, self.ny + 2, step, 0)


def patch(low, mid, high, y, x):
    pieces = []
    for ref in (low, mid, high):
        for ky in range(3):
            for kx in range(3):
                pieces.append(ref(y + ky, x + kx))
    return jnp.concatenate(pieces, axis=0)


def reader(ref, span=None):
    if span is None:
        return lambda y, x: ref[y, x]
    return lambda y, x: ref[y, x, span]


class Total:
    def __init__(self, at, sizes, refs, sems, owners, each):
        self.at, self.sizes, self.owners, self.each = at, sizes, owners, each
        self.terms, self.landed, self.held, self.result = refs
        self.sems = sems
        self.me = at[1] * sizes[2] + at[2]
        self.count = sizes[1] * sizes[2]

    def whole(self):
        return self.owners == self.count

    def when_owner(self, device, action):
        if self.whole():
            action()
        else:
            pl.when(device < self.owners)(action)

    def target(self, step):
        return lax.rem(self.me + step, self.count)

    def device(self, index):
        return (self.at[0], index // self.sizes[2], lax.rem(index, self.sizes[2]))

    def chunk(self, index):
        return pl.ds(index * self.each, self.each)

    def drain(self, ref, copies, sem):
        if copies:
            span = ref.at[pl.ds(0, copies)]
            pltpu.make_async_copy(span, span, self.sems.at[sem]).wait()

    def by_role(self, mine, others):
        if self.whole():
            mine()
        else:
            pl.when(self.me < self.owners)(mine)
            pl.when(self.me >= self.owners)(others)

    def start_scatter(self):
        for step in range(1, self.count):
            index = self.target(step)

            def send(step=step, index=index):
                pltpu.make_async_remote_copy(
                    src_ref=self.terms.at[self.chunk(index)],
                    dst_ref=self.landed.at[step - 1],
                    send_sem=self.sems.at[0],
                    recv_sem=self.sems.at[1],
                    device_id=self.device(index),
                    device_id_type=MESH,
                ).start()

            self.when_owner(index, send)

    def start_exchange(self):
        slab = self.at[0]

        def act():
            self.drain(self.landed, self.count - 1, 1)
            total = self.terms[self.chunk(self.me)].astype(F32)
            for step in range(self.count - 1):
                total = total + self.landed[step].astype(F32)
            self.held[slab] = total.astype(BF)
            for step in range(1, self.sizes[0]):
                pltpu.make_async_remote_copy(
                    src_ref=self.held.at[slab],
                    dst_ref=self.held.at[slab],
                    send_sem=self.sems.at[2],
                    recv_sem=self.sems.at[3],
                    device_id=(lax.rem(slab + step, self.sizes[0]), self.at[1], self.at[2]),
                    device_id_type=MESH,
                ).start()

        self.when_owner(self.me, act)

    def start_gather(self):
        def act():
            self.drain(self.held, self.sizes[0] - 1, 3)
            total = self.held[0].astype(F32)
            for step in range(1, self.sizes[0]):
                total = total + self.held[step].astype(F32)
            self.result[self.chunk(self.me)] = total.astype(BF)
            for step in range(1, self.count):
                pltpu.make_async_remote_copy(
                    src_ref=self.result.at[self.chunk(self.me)],
                    dst_ref=self.result.at[self.chunk(self.me)],
                    send_sem=self.sems.at[4],
                    recv_sem=self.sems.at[5],
                    device_id=self.device(self.target(step)),
                    device_id_type=MESH,
                ).start()

        self.when_owner(self.me, act)

    def finish(self):
        def mine():
            self.drain(self.terms, (self.owners - 1) * self.each, 0)
            self.drain(self.held, self.sizes[0] - 1, 2)
            self.drain(self.landed, self.count - 1, 4)
            self.drain(self.result, (self.owners - 1) * self.each, 5)

        def others():
            self.drain(self.terms, self.owners * self.each, 0)
            self.drain(self.result, self.owners * self.each, 5)

        self.by_role(mine, others)


def kernel(
    sizes,
    plan,
    feat_ref,
    cot_ref,
    enc_ref,
    down_ref,
    dec_ref,
    result_ref,
    grad_feat_ref,
    grad_enc_ref,
    grad_down_ref,
    grad_dec_ref,
    rows_ref,
    w_enc,
    w_enc_t,
    w_down,
    w_down_t,
    w_dec,
    w_dec_t,
    field_a,
    field_b,
    field_d,
    field_e,
    sent_a,
    sent_b,
    sent_d,
    sent_e,
    edge_a,
    edge_b,
    edge_d,
    edge_e,
    feat_low,
    feat_high,
    cot_low,
    cot_high,
    pool_low,
    pool_high,
    coarse_low,
    coarse_high,
    slope_low,
    slope_high,
    skip_low,
    skip_high,
    back_low,
    back_high,
    enc_pre,
    joined_grad,
    own_joined,
    dec_sum,
    enc_sum,
    terms_1,
    landed_1,
    held_1,
    result_1,
    terms_2,
    landed_2,
    held_2,
    result_2,
    halo_send,
    halo_recv,
    total_sems,
):
    (owners_1, each_1), (owners_2, each_2) = plan
    channels, nx, ny, _ = feat_ref.shape
    ncy = ny // 2
    coarse_channels = down_ref.shape[2]
    joined_channels = channels + coarse_channels
    at = (lax.axis_index("slab"), lax.axis_index("px"), lax.axis_index("py"))
    count = sizes[1] * sizes[2]
    sum_1 = Total(at, sizes, (terms_1, landed_1, held_1, result_1), total_sems.at[0], owners_1, each_1)
    sum_2 = Total(at, sizes, (terms_2, landed_2, held_2, result_2), total_sems.at[1], owners_2, each_2)

    for ref in (field_a, field_b, field_d, field_e, edge_a, edge_b, edge_d, edge_e):
        ref[...] = jnp.zeros_like(ref)

    barrier = pltpu.get_barrier_semaphore()
    for step in range(1, count):
        pl.semaphore_signal(barrier, inc=1, device_id=sum_1.device(sum_1.target(step)), device_id_type=MESH)
    for step in range(1, sizes[0]):
        other = lax.rem(at[0] + step, sizes[0])
        pl.semaphore_signal(barrier, inc=1, device_id=(other, at[1], at[2]), device_id_type=MESH)

    terms_1[...] = jnp.zeros_like(terms_1)
    terms_2[...] = jnp.zeros_like(terms_2)

    across = nx * ny
    for at_channel, ref in ((0, feat_ref), (channels, cot_ref)):
        rows_ref[...] = ref[...].astype(F32).reshape(channels * across, L)
        for x in range(nx):
            for y in range(ny):
                row = rows_ref[pl.ds(x * ny + y, channels, stride=across), :]
                field_a[y + 1, x + 1, at_channel : at_channel + channels] = row.astype(BF)

    pl.semaphore_wait(barrier, count - 1 + sizes[0] - 1)

    def halo(index, field, sent, edge, rows, columns, width):
        sems = (halo_send.at[index], halo_recv.at[index])
        return Halo(at, sizes, field, sent, edge, sems, rows, columns, width)

    halo_a = halo(0, field_a, sent_a, edge_a, ny, nx, 1)
    halo_b = halo(1, field_b, sent_b, edge_b, ncy, 1, 2)
    halo_d = halo(2, field_d, sent_d, edge_d, ncy, 1, 2)
    halo_e = halo(3, field_e, sent_e, edge_e, ny, nx, 1)

    halo_a.start_plane()
    w_enc[...] = jnp.concatenate([enc_ref[p] for p in PLACE], axis=1)
    w_enc_t[...] = jnp.concatenate([enc_ref[26 - p] for p in PLACE], axis=0).T
    w_down[...] = jnp.concatenate([down_ref[p] for p in PLACE], axis=0).T
    w_down_t[...] = jnp.concatenate([down_ref[26 - p] for p in PLACE], axis=1)
    w_dec[...] = jnp.concatenate([dec_ref[p] for p in PLACE], axis=1)
    w_dec_t[...] = jnp.concatenate([dec_ref[26 - p] for p in PLACE], axis=0).T
    halo_a.wait_plane()
    halo_a.start_depth()
    halo_a.wait_depth()
    head, tail = slice(0, channels), slice(channels, 2 * channels)
    halo_a.shift(head, feat_low, feat_high, 1)
    halo_a.shift(tail, cot_low, cot_high, 1)
    feat_of = (reader(feat_low), reader(field_a, head), reader(feat_high))
    cot_of = (reader(cot_low), reader(field_a, tail), reader(cot_high))

    def fine(of, y):
        return jnp.concatenate([patch(*of, y, x) for x in range(nx)], axis=1)

    def span_of(y):
        return pl.ds(pl.multiple_of(y * (nx * L), nx * L), nx * L)

    def encode(yc, carry):
        pooled = jnp.zeros((channels, L), F32)
        for sub in range(2):
            y = 2 * yc + sub
            pre = dot(w_enc[...], fine(feat_of, y))
            enc_pre[:, span_of(y)] = pre
            skip = (pre * jax.nn.sigmoid(pre)).astype(BF)
            own_joined[coarse_channels:, span_of(y)] = skip
            for x in range(nx):
                row = skip[:, x * L : (x + 1) * L]
                field_e[y + 1, x + 1, head] = row
                pooled = pooled + row.astype(F32)
        field_b[yc + 1, 1] = (pair_sum(pooled) * 0.125).astype(BF)
        return carry

    lax.fori_loop(0, ncy, encode, 0)

    halo_b.start_plane()

    def back(y, carry):
        joined_grad[:, span_of(y)] = dot(w_dec_t[...], fine(cot_of, y))
        return carry

    lax.fori_loop(0, ny, back, 0)
    halo_b.wait_plane()
    halo_b.start_depth()
    halo_b.wait_depth()
    halo_b.shift(slice(0, channels), pool_low, pool_high, 2)
    pool_of = (reader(pool_low), reader(field_b), reader(pool_high))
    pooled_patch = jnp.concatenate([patch(*pool_of, yc, 0) for yc in range(ncy)], axis=1)
    down_pre = dot(w_down[...], pooled_patch)
    coarse = (down_pre * jax.nn.sigmoid(down_pre)).astype(BF)
    slope = silu_slope(down_pre)
    low_half, high_half = slice(0, coarse_channels), slice(coarse_channels, 2 * coarse_channels)
    grads = []
    for yc in range(ncy):
        field_d[yc + 1, 1, low_half] = coarse[:, yc * L : (yc + 1) * L]
        folded = jnp.zeros((coarse_channels, L), F32)
        for sub in range(2):
            for x in range(nx):
                cell = ((2 * yc + sub) * nx + x) * L
                folded = folded + joined_grad[:coarse_channels, cell : cell + L]
                own_joined[:coarse_channels, cell : cell + L] = coarse[:, yc * L : (yc + 1) * L]
        grad = (pair_sum(folded) * slope[:, yc * L : (yc + 1) * L]).astype(BF)
        field_d[yc + 1, 1, high_half] = grad
        grads.append(grad)

    halo_d.start_plane()
    down_sum = dot_t(pooled_patch, jnp.concatenate(grads, axis=1)) * 0.5
    half = down_sum.shape[0] // 2
    dec_sum[...] = jnp.zeros_like(dec_sum)

    def dec_step(y, carry):
        dec_sum[...] += dot_t(fine(cot_of, y), own_joined[:, span_of(y)])
        return carry

    lax.fori_loop(0, ny, dec_step, 0)
    dec_tiles = dec_sum.shape[0] // 16
    down_tiles = half // 16
    terms_1[0:dec_tiles, :, 0:joined_channels] = dec_sum[...].astype(BF).reshape(dec_tiles, 16, joined_channels)
    paired = jnp.concatenate([down_sum[:half], down_sum[half:]], axis=1)
    terms_1[dec_tiles : dec_tiles + down_tiles] = paired.astype(BF).reshape(down_tiles, 16, L)
    halo_d.wait_plane()
    halo_d.start_depth()
    sum_1.start_scatter()
    halo_d.wait_depth()
    halo_d.shift(high_half, slope_low, slope_high, 2)
    slope_of = (reader(slope_low), reader(field_d, high_half), reader(slope_high))
    slope_patch = jnp.concatenate([patch(*slope_of, yc, 0) for yc in range(ncy)], axis=1)
    grad_pooled = dot(w_down_t[...], slope_patch) * 0.125
    for yc in range(ncy):
        for sub in range(2):
            for x in range(nx):
                cell = ((2 * yc + sub) * nx + x) * L
                total = joined_grad[coarse_channels:, cell : cell + L] + grad_pooled[:, yc * L : (yc + 1) * L]
                grad = (total * silu_slope(enc_pre[:, cell : cell + L])).astype(BF)
                field_e[2 * yc + sub + 1, x + 1, tail] = grad

    halo_e.start_plane()
    enc_sum[...] = jnp.zeros_like(enc_sum)

    def enc_step(y, carry):
        own = jnp.concatenate([field_e[y + 1, x + 1, tail] for x in range(nx)], axis=1)
        enc_sum[...] += dot_t(own, fine(feat_of, y))
        return carry

    lax.fori_loop(0, ny, enc_step, 0)
    wide = enc_sum.shape[1]
    for h in range(channels // 16):
        for at_lane in range(0, wide, L):
            size = min(L, wide - at_lane)
            piece = enc_sum[16 * h : 16 * h + 16, at_lane : at_lane + size]
            terms_2[h * pl.cdiv(wide, L) + at_lane // L, :, 0:size] = piece.astype(BF)
    sum_2.start_scatter()
    halo_d.shift(low_half, coarse_low, coarse_high, 1)
    halo_e.wait_plane()
    halo_e.start_depth()
    sum_1.start_exchange()
    sum_2.start_exchange()
    halo_e.wait_depth()
    halo_e.shift(tail, back_low, back_high, 1)
    halo_e.shift(head, skip_low, skip_high, 1)
    sum_1.start_gather()
    sum_2.start_gather()

    back_of = (reader(back_low), reader(field_e, tail), reader(back_high))

    def put(y, value):
        for x in range(nx):
            rows_ref[pl.ds(x * ny + y, channels, stride=across), :] = value[:, x * L : (x + 1) * L]

    def flush(ref):
        ref[...] = rows_ref[...].reshape(channels, nx, ny, L).astype(BF)

    def feat_step(y, carry):
        put(y, dot(w_enc_t[...], fine(back_of, y)))
        return carry

    lax.fori_loop(0, ny, feat_step, 0)
    flush(grad_feat_ref)

    coarse_of = (reader(coarse_low), reader(field_d, low_half), reader(coarse_high))
    skip_of = (reader(skip_low), reader(field_e, head), reader(skip_high))

    def result_step(yc, carry):
        for sub in range(2):
            columns = []
            for x in range(nx):
                pieces = []
                for kz in range(3):
                    for ky in range(3):
                        for kx in range(3):
                            pieces.append(coarse_of[kz](yc + (sub + ky + 1) // 2, (x + kx + 1) // 2))
                            pieces.append(skip_of[kz](2 * yc + sub + ky, x + kx))
                columns.append(jnp.concatenate(pieces, axis=0))
            put(2 * yc + sub, dot(w_dec[...], jnp.concatenate(columns, axis=1)))
        return carry

    lax.fori_loop(0, ncy, result_step, 0)
    flush(result_ref)

    scale = 1.0 / math.sqrt(float(nx * ny * L * sizes[0] * sizes[1] * sizes[2]))
    sum_1.finish()
    tiles = channels // 16
    for index, (place) in enumerate(PLACE):
        held = result_1[index * tiles : (index + 1) * tiles].astype(F32).reshape(channels, L)
        grad_dec_ref[26 - place] = held[:, :joined_channels] * scale
    both = result_1[dec_tiles : dec_tiles + down_tiles].astype(F32).reshape(half, L) * scale
    whole = jnp.concatenate([both[:, :coarse_channels], both[:, coarse_channels:]], axis=0)
    for index, place in enumerate(PLACE):
        grad_down_ref[place] = whole[index * channels : (index + 1) * channels]
    sum_2.finish()
    across_tiles = pl.cdiv(wide, L)
    for index, place in enumerate(PLACE):
        lane = index * channels
        for h in range(channels // 16):
            tile = result_2[h * across_tiles + lane // L].astype(F32)
            grad_enc_ref[place, 16 * h : 16 * h + 16] = tile[:, lane % L : lane % L + channels] * scale
    for each in (halo_a, halo_b, halo_d, halo_e):
        each.wait_sent()


def shards(sizes, feat, w_enc, w_down, w_dec, cotangent):
    channels, nx, ny, nz = feat.shape
    coarse_channels = w_down.shape[0]
    joined_channels = channels + coarse_channels
    ncy = ny // 2
    count = sizes[1] * sizes[2]
    tiles_1 = 27 * channels // 16 + 27 * channels // 32
    tiles_2 = channels // 16 * pl.cdiv(27 * channels, L)
    owners_1, owners_2 = count, min(count, tiles_2)
    each_1, each_2 = pl.cdiv(tiles_1, owners_1), pl.cdiv(tiles_2, owners_2)

    def taps(weight, order):
        return weight.transpose(2, 3, 4, *order).reshape(27, weight.shape[order[0]], weight.shape[order[1]])

    def vmem(*shape, dtype=BF):
        return pltpu.VMEM(shape, dtype)

    def fine(c):
        return vmem(ny + 2, nx + 2, c, L)

    def small(c):
        return vmem(ncy + 2, 3, c, L)

    c1, c2, cj = channels, coarse_channels, joined_channels
    scratch = [
        vmem(c1 * nx * ny, L, dtype=F32),
        vmem(c1, 27 * c1),
        vmem(c1, 27 * c1),
        vmem(c2, 27 * c1),
        vmem(c1, 27 * c2),
        vmem(c1, 27 * cj),
        vmem(cj, 27 * c1),
        fine(2 * c1),
        small(c1),
        small(2 * c2),
        fine(2 * c1),
    ]
    scratch += [vmem(2, c, L) for c in (2 * c1, c1, 2 * c2, 2 * c1)] * 2
    scratch += [fine(c1)] * 4 + [small(c1)] * 2 + [small(c2)] * 4 + [fine(c1)] * 4
    scratch += [
        vmem(c1, nx * ny * L, dtype=F32),
        vmem(cj, nx * ny * L, dtype=F32),
        vmem(cj, nx * ny * L),
        vmem(27 * c1, cj, dtype=F32),
        vmem(c1, 27 * c1, dtype=F32),
    ]
    for owners, each in ((owners_1, each_1), (owners_2, each_2)):
        scratch += [
            vmem(owners * each, 16, L),
            vmem(count - 1, each, 16, L),
            vmem(sizes[0], each, 16, L),
            vmem(owners * each, 16, L),
        ]
    scratch += [
        pltpu.SemaphoreType.DMA((4, 10)),
        pltpu.SemaphoreType.DMA((4, 10)),
        pltpu.SemaphoreType.DMA((2, 6)),
    ]
    whole = pl.BlockSpec(memory_space=pltpu.VMEM)
    shapes = [
        jax.ShapeDtypeStruct(feat.shape, BF),
        jax.ShapeDtypeStruct(feat.shape, BF),
        jax.ShapeDtypeStruct((27, c1, c1), F32),
        jax.ShapeDtypeStruct((27, c1, c2), F32),
        jax.ShapeDtypeStruct((27, c1, cj), F32),
    ]
    result, grad_feat, grad_enc, grad_down, grad_dec = pl.pallas_call(
        functools.partial(kernel, sizes, ((owners_1, each_1), (owners_2, each_2))),
        out_shape=shapes,
        in_specs=[whole] * 5,
        out_specs=[whole] * 5,
        scratch_shapes=scratch,
        compiler_params=pltpu.CompilerParams(
            collective_id=0, has_side_effects=True, vmem_limit_bytes=56 << 20
        ),
    )(feat, cotangent, taps(w_enc, (0, 1)), taps(w_down, (1, 0)), taps(w_dec, (0, 1)))

    def untaps(value, order):
        return value.reshape(3, 3, 3, *value.shape[1:]).transpose(*order, 0, 1, 2)

    return (
        result,
        grad_feat,
        untaps(grad_enc, (3, 4)),
        untaps(grad_down, (4, 3)),
        untaps(grad_dec, (3, 4)),
    )


def solution(mesh):
    sizes = tuple(mesh.shape[axis] for axis in ("slab", "px", "py"))
    placed = P(None, "px", "py", "slab")
    return jax.shard_map(
        functools.partial(shards, sizes),
        mesh=mesh,
        in_specs=(placed, P(), P(), P(), placed),
        out_specs=(placed, placed, P(), P(), P()),
        check_vma=False,
    )
```

time: 582 us -> 74.9 us (0.13); the launches traced: 573 us -> 74.6 us
  waiting for transfers between devices: 271 us -> 0 us
  starting transfers between devices: 121 us -> 0 us
  Pallas kernels: 0 us -> 67.7 us
  blocking collectives: 46.3 us -> 0 us
  local copies, waits for them, and re-layouts: 49.8 us -> 6.3 us
  matrix products: 42.5 us -> 0 us
  other arithmetic: 26.8 us -> 0 us
  between operations: 15.8 us -> 0.65 us
    psum x1 -> x0, waiting for transfers between devices: 266 us -> none  [shards(): lax.psum((enc_sum, down_sum, dec_sum), ('slab', 'px', 'py'))]
    ppermute x32 -> x0, starting transfers between devices: 121 us -> none  [the longest x16 82.9 us: padded_2(): lax.ppermute(lax.slice_in_dim(block, block.shape[dim] - width, None, axis...]
    pallas_call x0 -> x1, Pallas kernels: none -> 67.7 us  [shards(): pl.pallas_call(functools.partial(kernel, sizes, ((owners_1, each_1), (own...]
    all_gather x2 -> x0, blocking collectives: 46.3 us -> none  [the longest x1 23.4 us: shards(): grad_all = lax.all_gather(grad_coarse, 'py', axis=2, tiled=True)]
    unnamed x91 -> x11, local copies, waits for them, and re-layouts: 29.2 us -> 6.3 us
    dot_general x81 -> x0, matrix products: 22.4 us -> none  [weight_grad(): jnp.einsum('oxyz,ixyz->oi', grad_out, piece, preferred_element_type=jnp.f...]
    conv_general_dilated x6 -> x0, matrix products: 20.1 us -> none  [conv_valid(): lax.conv_general_dilated(padded[None], weight, (1, 1, 1), 'VALID', dimens...]
    concatenate x12 -> x0, other arithmetic: 11 us -> none  [the longest x11 10.9 us: padded_2(): block = jnp.concatenate([low, block, high], axis=dim)]
  transfers between devices with their start and end apart: 33 -> 0, of which waited for: 5 -> 0; matrix products, arithmetic and copies ran while one was open for 9% -> 0% of each run, Pallas kernels for 0% -> 0%
where the time goes in v1:
time: 74.9 us; the launch traced here: 74.6 us
  Pallas kernels  67.7 us (90%)
  local copies, waits for them, and re-layouts  6.3 us (8%)
    pallas_call x1, Pallas kernels, shards(): pl.pallas_call(functools.partial(kernel, sizes, ((owners_1, each_1), (own...  67.7 us
    unnamed x11, local copies, waits for them, and re-layouts  6.3 us

profile of v1, /device:TPU:1, one launch (start us, length us, event | category | flops | bytes accessed | tf_op | source)
XLA Modules:
  0.0 74.6 jit_solution(3977189581882714067)
XLA Ops:
  0.6 67.7 %shard_map.92 = (bf16[32,2,8,128]{3,2,1,0:T(8,128)(2,1)}, bf16[32,2,8,128]{3,2,1,0:T(8,128)(2,1)}, f32[27,32,32]{2,1,0:T(8,128)}, f32[27,32,64]{2,1,0:T(8,128)}, f32[27,32,96]{2,1,0:T(8,128)}) custom-call(bf16[32,2,8,128]{3,2,1,0:T(8,128)(2,1)} %feat_ref.1, bf16[32,2,8,128]{3,2,1,0:T(8,128)(2,1)} %cot_ref.1, bf16[27,32,32]{2,1,0:T(8,128)(2,1)} %bitcast.21, ...), custom_call_target="tpu_custom_call" | custom-call | tf_op jit(solution)/shard_map/pallas_call | solution.py:623
  68.3 0.0 copy-start.2
  68.3 1.6 %copy.15 = bf16[32,2,8,128]{3,2,1,0:T(8,128)(2,1)} copy(bf16[32,2,8,128]{3,2,1,0:T(8,128)(2,1)} %get-tuple-element.20) | data formatting | bytes 262144
  69.9 1.6 %copy.16 = bf16[32,2,8,128]{3,2,1,0:T(8,128)(2,1)} copy(bf16[32,2,8,128]{3,2,1,0:T(8,128)(2,1)} %get-tuple-element.21) | data formatting | bytes 262144
  71.5 0.0 copy-done.2
  71.5 0.0 copy-start.1
  71.5 0.8 %copy.17 = f32[32,32,3,3,3]{1,0,4,3,2:T(8,128)} copy(f32[32,32,3,3,3]{1,0,4,3,2:T(8,128)S(1)} %bitcast.20) | data formatting | bytes 221184
  72.3 0.4 copy-done.1
  72.7 0.0 copy-start
  72.7 0.8 %copy.18 = f32[64,32,3,3,3]{0,1,4,3,2:T(8,128)} copy(f32[64,32,3,3,3]{0,1,4,3,2:T(8,128)S(1)} %bitcast.19) | data formatting | bytes 442368
  73.4 0.4 copy-done
  73.9 0.8 %copy.19 = f32[32,96,3,3,3]{1,0,4,3,2:T(8,128)} copy(f32[32,96,3,3,3]{1,0,4,3,2:T(8,128)S(1)} %bitcast.18) | data formatting | bytes 663552
Async XLA Ops:
  68.3 3.2 %copy-start.2 = (f32[27,32,32]{2,1,0:T(8,128)S(1)}, f32[27,32,32]{2,1,0:T(8,128)}, u32[]{:S(2)}) copy-start(f32[27,32,32]{2,1,0:T(8,128)} %get-tuple-element.12) | copy-start | bytes 331780
  71.5 1.2 %copy-start.1 = (f32[27,32,64]{2,1,0:T(8,128)S(1)}, f32[27,32,64]{2,1,0:T(8,128)}, u32[]{:S(2)}) copy-start(f32[27,32,64]{2,1,0:T(8,128)} %get-tuple-element.13) | copy-start | bytes 663556
  72.7 1.2 %copy-start = (f32[27,32,96]{2,1,0:T(8,128)S(1)}, f32[27,32,96]{2,1,0:T(8,128)}, u32[]{:S(2)}) copy-start(f32[27,32,96]{2,1,0:T(8,128)} %get-tuple-element.14) | copy-start | bytes 995332

commit v2 on v1

v2 whole, which is shorter than its diff:
```python
import functools
import itertools
import math

import jax
import jax.numpy as jnp
from jax import lax
from jax.experimental import pallas as pl
from jax.experimental.pallas import tpu as pltpu
from jax.sharding import PartitionSpec as P

EXCHANGES = ("feat", "cot", "pool", "skip", "slope", "coarse", "back")
FINE = (0, 1, 3, 6)
MESH = pl.DeviceIdType.MESH
BF = jnp.bfloat16
F32 = jnp.float32
L = 128
TAPS = [(kx, ky, kz) for kz in range(3) for ky in range(3) for kx in range(3)]
PLACE = [kx * 9 + ky * 3 + kz for kx, ky, kz in TAPS]
AROUND = sorted(
    (step for step in itertools.product((-1, 0, 1), repeat=3) if any(step)),
    key=lambda step: -sum(map(abs, step)),
)


def dot(a, b):
    return jnp.dot(a, b, preferred_element_type=F32)


def dot_t(a, b):
    return lax.dot_general(a, b, (((1,), (1,)), ((), ())), preferred_element_type=F32)


def lanes():
    return lax.broadcasted_iota(jnp.int32, (1, L), 1)


def pair_sum(value):
    even = lax.rem(lanes(), 2) == 0
    return value + jnp.where(even, pltpu.roll(value, L - 1, 1), pltpu.roll(value, 1, 1))


def silu_slope(value):
    sig = jax.nn.sigmoid(value)
    return sig * (1.0 + value * (1.0 - sig))


def near(at, sizes, step, sign=1):
    inside = True
    for place, size, move in zip(at, sizes, step):
        if move:
            inside = inside & (place + sign * move >= 0) & (place + sign * move < size)
    return inside


class Halo:
    def __init__(self, at, sizes, field, sent, edge, sems, ny, nx, width):
        self.at, self.sizes, self.field, self.sent, self.edge = at, sizes, field, sent, edge
        self.send, self.recv = sems
        self.ny, self.nx, self.width = ny, nx, width

    def has(self, step, sign=1):
        return near(self.at, self.sizes, step, sign)

    def copy(self, index):
        ds, dx, dy = AROUND[index]

        def spans(step, size):
            source = {-1: pl.ds(1, 1), 0: pl.ds(1, size), 1: pl.ds(size, 1)}[step]
            target = {-1: pl.ds(size + 1, 1), 0: pl.ds(1, size), 1: pl.ds(0, 1)}[step]
            return source, target

        if ds == 0:
            (sx, tx), (sy, ty) = spans(dx, self.nx), spans(dy, self.ny)
            source, target = self.field.at[sy, sx], self.field.at[ty, tx]
        else:
            side = (1 - ds) // 2
            source, target = self.sent.at[side], self.edge.at[side, (1 - dy) * 3 + 1 - dx]
        return pltpu.make_async_remote_copy(
            src_ref=source,
            dst_ref=target,
            send_sem=self.send.at[index],
            recv_sem=self.recv.at[index],
            device_id=tuple(a + d for a, d in zip(self.at, AROUND[index])),
            device_id_type=MESH,
        )

    def start_where(self, plane):
        for index, step in enumerate(AROUND):
            if (step[0] == 0) == plane:
                pl.when(self.has(step))(lambda index=index: self.copy(index).start())

    def place(self, group, cell):
        return self.width * ((group * self.ny + cell[0]) * self.nx + cell[1])

    def start(self):
        self.start_where(True)
        width = self.width
        lane = lanes() // width
        last = first = jnp.zeros((16, L), F32)
        for cell in itertools.product(range(self.ny), range(self.nx)):
            row = self.field[cell[0] + 1, cell[1] + 1].astype(F32)
            for group in range(row.shape[0] // 16):
                piece = row[16 * group : 16 * group + 16]
                place = self.place(group, cell)
                here = lane == place // width
                last = jnp.where(here, pltpu.roll(piece, (place + width) % L, 1), last)
                first = jnp.where(here, pltpu.roll(piece, place, 1), first)
        self.sent[0] = last.astype(BF)
        self.sent[1] = first.astype(BF)
        self.start_where(False)

    def clear(self):
        zero = jnp.zeros(self.field.shape[2:], BF)
        for y in range(self.ny + 2):
            for x in range(self.nx + 2):
                if y in (0, self.ny + 1) or x in (0, self.nx + 1):
                    self.field[y, x] = zero
        self.edge[...] = jnp.zeros_like(self.edge)

    def wait(self):
        for index, step in enumerate(AROUND):
            pl.when(self.has(step, -1))(lambda index=index: self.copy(index).wait_recv())

    def wait_sent(self):
        for index, step in enumerate(AROUND):
            pl.when(self.has(step))(lambda index=index: self.copy(index).wait_send())

    def shift(self, low, high, by):
        ny, nx = self.ny, self.nx
        lane = lanes()
        for y in range(ny + 2):
            for x in range(nx + 2):
                row = self.field[y, x].astype(F32)
                (dy, oy), (dx, ox) = divmod(y + ny - 1, ny), divmod(x + nx - 1, nx)
                left = self.edge[0, dy * 3 + dx].astype(F32)
                right = self.edge[1, dy * 3 + dx].astype(F32)
                places = [self.place(group, (oy, ox)) for group in range(row.shape[0] // 16)]
                first = jnp.concatenate([pltpu.roll(left, (L - at) % L, 1) for at in places])
                last = jnp.concatenate([pltpu.roll(right, (2 * L - by - at) % L, 1) for at in places])
                low[y, x] = jnp.where(lane < by, first, pltpu.roll(row, by, 1)).astype(BF)
                high[y, x] = jnp.where(lane >= L - by, last, pltpu.roll(row, L - by, 1)).astype(BF)


def patch(low, mid, high, y, x):
    pieces = []
    for ref in (low, mid, high):
        for ky in range(3):
            for kx in range(3):
                pieces.append(ref(y + ky, x + kx))
    return jnp.concatenate(pieces, axis=0)


def reader(ref):
    return lambda y, x: ref[y, x]


class Total:
    def __init__(self, at, sizes, refs, sems, owners, each):
        self.at, self.sizes, self.owners, self.each = at, sizes, owners, each
        self.terms, self.landed, self.held, self.result = refs
        self.sems = sems
        self.me = at[1] * sizes[2] + at[2]
        self.count = sizes[1] * sizes[2]

    def whole(self):
        return self.owners == self.count

    def when_owner(self, device, action):
        if self.whole():
            action()
        else:
            pl.when(device < self.owners)(action)

    def target(self, step):
        return lax.rem(self.me + step, self.count)

    def device(self, index):
        return (self.at[0], index // self.sizes[2], lax.rem(index, self.sizes[2]))

    def chunk(self, index):
        return pl.ds(index * self.each, self.each)

    def drain(self, ref, copies, sem):
        if copies:
            span = ref.at[pl.ds(0, copies)]
            pltpu.make_async_copy(span, span, self.sems.at[sem]).wait()

    def by_role(self, mine, others):
        if self.whole():
            mine()
        else:
            pl.when(self.me < self.owners)(mine)
            pl.when(self.me >= self.owners)(others)

    def start_scatter(self):
        for step in range(1, self.count):
            index = self.target(step)

            def send(step=step, index=index):
                pltpu.make_async_remote_copy(
                    src_ref=self.terms.at[self.chunk(index)],
                    dst_ref=self.landed.at[step - 1],
                    send_sem=self.sems.at[0],
                    recv_sem=self.sems.at[1],
                    device_id=self.device(index),
                    device_id_type=MESH,
                ).start()

            self.when_owner(index, send)

    def start_exchange(self):
        slab = self.at[0]

        def act():
            self.drain(self.landed, self.count - 1, 1)
            total = self.terms[self.chunk(self.me)].astype(F32)
            for step in range(self.count - 1):
                total = total + self.landed[step].astype(F32)
            self.held[slab] = total.astype(BF)
            for step in range(1, self.sizes[0]):
                pltpu.make_async_remote_copy(
                    src_ref=self.held.at[slab],
                    dst_ref=self.held.at[slab],
                    send_sem=self.sems.at[2],
                    recv_sem=self.sems.at[3],
                    device_id=(lax.rem(slab + step, self.sizes[0]), self.at[1], self.at[2]),
                    device_id_type=MESH,
                ).start()

        self.when_owner(self.me, act)

    def start_gather(self):
        def act():
            self.drain(self.held, self.sizes[0] - 1, 3)
            total = self.held[0].astype(F32)
            for step in range(1, self.sizes[0]):
                total = total + self.held[step].astype(F32)
            self.result[self.chunk(self.me)] = total.astype(BF)
            for step in range(1, self.count):
                pltpu.make_async_remote_copy(
                    src_ref=self.result.at[self.chunk(self.me)],
                    dst_ref=self.result.at[self.chunk(self.me)],
                    send_sem=self.sems.at[4],
                    recv_sem=self.sems.at[5],
                    device_id=self.device(self.target(step)),
                    device_id_type=MESH,
                ).start()

        self.when_owner(self.me, act)

    def finish(self):
        def mine():
            self.drain(self.terms, (self.owners - 1) * self.each, 0)
            self.drain(self.held, self.sizes[0] - 1, 2)
            self.drain(self.landed, self.count - 1, 4)
            self.drain(self.result, (self.owners - 1) * self.each, 5)

        def others():
            self.drain(self.terms, self.owners * self.each, 0)
            self.drain(self.result, self.owners * self.each, 5)

        self.by_role(mine, others)


def kernel(
    sizes,
    plan,
    feat_in,
    cot_in,
    enc_in,
    down_in,
    dec_in,
    result_out,
    grad_feat_out,
    tiles_1_out,
    tiles_2_out,
    feat_ref,
    cot_ref,
    enc_ref,
    down_ref,
    dec_ref,
    result_ref,
    grad_feat_ref,
    rows_ref,
    w_enc,
    w_enc_t,
    w_down,
    w_down_t,
    w_dec,
    w_dec_t,
    fields,
    lows,
    highs,
    sents,
    edges,
    enc_pre,
    joined_grad,
    own_joined,
    dec_sum,
    enc_sum,
    total_refs_1,
    total_refs_2,
    halo_send,
    halo_recv,
    total_sems,
    sems,
):
    (owners_1, each_1), (owners_2, each_2) = plan
    channels, nx, ny, _ = feat_ref.shape
    ncy = ny // 2
    coarse_channels = down_ref.shape[2]
    joined_channels = channels + coarse_channels
    at = (lax.axis_index("slab"), lax.axis_index("px"), lax.axis_index("py"))
    count = sizes[1] * sizes[2]
    sum_1 = Total(at, sizes, total_refs_1, total_sems.at[0], owners_1, each_1)
    sum_2 = Total(at, sizes, total_refs_2, total_sems.at[1], owners_2, each_2)

    arrive = [
        pltpu.make_async_copy(source, target, sems.at[index])
        for index, (source, target) in enumerate(
            zip((feat_in, cot_in, enc_in, down_in, dec_in), (feat_ref, cot_ref, enc_ref, down_ref, dec_ref))
        )
    ]
    for copy in arrive:
        copy.start()

    def halo(index, rows, columns, width):
        refs = (fields[index], sents[index], edges[index])
        return Halo(at, sizes, *refs, (halo_send.at[index], halo_recv.at[index]), rows, columns, width)

    halos = [halo(index, *((ny, nx, 1) if index in FINE else (ncy, 1, 2))) for index in range(7)]
    of_feat, of_cot, of_pool, of_skip, of_slope, of_coarse, of_back = halos
    for each in halos:
        each.clear()

    barrier = pltpu.get_barrier_semaphore()
    for step in range(1, count):
        pl.semaphore_signal(barrier, inc=1, device_id=sum_1.device(sum_1.target(step)), device_id_type=MESH)
    for step in range(1, sizes[0]):
        other = lax.rem(at[0] + step, sizes[0])
        pl.semaphore_signal(barrier, inc=1, device_id=(other, at[1], at[2]), device_id_type=MESH)
    greeted = count - 1 + sizes[0] - 1
    for step in AROUND:
        if step[0] and (step[1] or step[2]):
            there = near(at, sizes, step)
            greeted = greeted + there.astype(jnp.int32)
            target = tuple(a + d for a, d in zip(at, step))

            @pl.when(there)
            def _(target=target):
                pl.semaphore_signal(barrier, inc=1, device_id=target, device_id_type=MESH)

    across = nx * ny
    for index, ref in ((0, feat_ref), (1, cot_ref)):
        arrive[index].wait()
        rows_ref[...] = ref[...].astype(F32).reshape(channels * across, L)
        for x in range(nx):
            for y in range(ny):
                row = rows_ref[pl.ds(x * ny + y, channels, stride=across), :]
                fields[index][y + 1, x + 1] = row.astype(BF)
    terms_1, terms_2 = total_refs_1[0], total_refs_2[0]
    terms_1[...] = jnp.zeros_like(terms_1)
    terms_2[...] = jnp.zeros_like(terms_2)
    pl.semaphore_wait(barrier, greeted)

    of_feat.start()
    of_cot.start()
    for copy in arrive[2:]:
        copy.wait()
    w_enc[...] = jnp.concatenate([enc_ref[p] for p in PLACE], axis=1)
    w_enc_t[...] = jnp.concatenate([enc_ref[26 - p] for p in PLACE], axis=0).T
    w_down[...] = jnp.concatenate([down_ref[p] for p in PLACE], axis=0).T
    w_down_t[...] = jnp.concatenate([down_ref[26 - p] for p in PLACE], axis=1)
    w_dec[...] = jnp.concatenate([dec_ref[p] for p in PLACE], axis=1)
    w_dec_t[...] = jnp.concatenate([dec_ref[26 - p] for p in PLACE], axis=0).T

    def moved(index, by):
        halos[index].shift(lows[index], highs[index], by)
        return reader(lows[index]), reader(fields[index]), reader(highs[index])

    def fine(of, y):
        return jnp.concatenate([patch(*of, y, x) for x in range(nx)], axis=1)

    def span_of(y):
        return pl.ds(pl.multiple_of(y * (nx * L), nx * L), nx * L)

    of_feat.wait()
    feat_of = moved(0, 1)

    def encode(yc, carry):
        pooled = jnp.zeros((channels, L), F32)
        for sub in range(2):
            y = 2 * yc + sub
            pre = dot(w_enc[...], fine(feat_of, y))
            enc_pre[:, span_of(y)] = pre
            skip = (pre * jax.nn.sigmoid(pre)).astype(BF)
            own_joined[coarse_channels:, span_of(y)] = skip
            for x in range(nx):
                row = skip[:, x * L : (x + 1) * L]
                fields[3][y + 1, x + 1] = row
                pooled = pooled + row.astype(F32)
        fields[2][yc + 1, 1] = (pair_sum(pooled) * 0.125).astype(BF)
        return carry

    lax.fori_loop(0, ncy, encode, 0)

    of_pool.start()
    of_skip.start()
    of_cot.wait()
    cot_of = moved(1, 1)

    def back(y, carry):
        joined_grad[:, span_of(y)] = dot(w_dec_t[...], fine(cot_of, y))
        return carry

    lax.fori_loop(0, ny, back, 0)
    of_pool.wait()
    pool_of = moved(2, 2)
    pooled_patch = jnp.concatenate([patch(*pool_of, yc, 0) for yc in range(ncy)], axis=1)
    down_pre = dot(w_down[...], pooled_patch)
    slope = silu_slope(down_pre)
    grads = []
    for yc in range(ncy):
        folded = jnp.zeros((coarse_channels, L), F32)
        for sub in range(2):
            for x in range(nx):
                cell = ((2 * yc + sub) * nx + x) * L
                folded = folded + joined_grad[:coarse_channels, cell : cell + L]
        grad = (pair_sum(folded) * slope[:, yc * L : (yc + 1) * L]).astype(BF)
        fields[4][yc + 1, 1] = grad
        grads.append(grad)

    of_slope.start()
    coarse = (down_pre * jax.nn.sigmoid(down_pre)).astype(BF)
    for yc in range(ncy):
        own = coarse[:, yc * L : (yc + 1) * L]
        fields[5][yc + 1, 1] = own
        for sub in range(2):
            for x in range(nx):
                cell = ((2 * yc + sub) * nx + x) * L
                own_joined[:coarse_channels, cell : cell + L] = own
    of_coarse.start()
    down_sum = dot_t(pooled_patch, jnp.concatenate(grads, axis=1)) * 0.5
    half = down_sum.shape[0] // 2
    dec_sum[...] = jnp.zeros_like(dec_sum)

    def dec_step(y, carry):
        dec_sum[...] += dot_t(fine(cot_of, y), own_joined[:, span_of(y)])
        return carry

    lax.fori_loop(0, ny, dec_step, 0)
    dec_tiles = dec_sum.shape[0] // 16
    down_tiles = half // 16
    terms_1[0:dec_tiles, :, 0:joined_channels] = dec_sum[...].astype(BF).reshape(dec_tiles, 16, joined_channels)
    paired = jnp.concatenate([down_sum[:half], down_sum[half:]], axis=1)
    terms_1[dec_tiles : dec_tiles + down_tiles] = paired.astype(BF).reshape(down_tiles, 16, L)
    sum_1.start_scatter()
    of_slope.wait()
    slope_of = moved(4, 2)
    slope_patch = jnp.concatenate([patch(*slope_of, yc, 0) for yc in range(ncy)], axis=1)
    grad_pooled = dot(w_down_t[...], slope_patch) * 0.125
    for yc in range(ncy):
        for sub in range(2):
            for x in range(nx):
                cell = ((2 * yc + sub) * nx + x) * L
                total = joined_grad[coarse_channels:, cell : cell + L] + grad_pooled[:, yc * L : (yc + 1) * L]
                grad = (total * silu_slope(enc_pre[:, cell : cell + L])).astype(BF)
                fields[6][2 * yc + sub + 1, x + 1] = grad

    enc_sum[...] = jnp.zeros_like(enc_sum)

    def enc_step(y, carry):
        own = jnp.concatenate([fields[6][y + 1, x + 1] for x in range(nx)], axis=1)
        enc_sum[...] += dot_t(own, fine(feat_of, y))
        return carry

    lax.fori_loop(0, ny, enc_step, 0)
    wide = enc_sum.shape[1]
    for h in range(channels // 16):
        for at_lane in range(0, wide, L):
            size = min(L, wide - at_lane)
            piece = enc_sum[16 * h : 16 * h + 16, at_lane : at_lane + size]
            terms_2[h * pl.cdiv(wide, L) + at_lane // L, :, 0:size] = piece.astype(BF)
    sum_2.start_scatter()
    of_back.start()
    sum_1.start_exchange()

    def put(y, value):
        for x in range(nx):
            rows_ref[pl.ds(x * ny + y, channels, stride=across), :] = value[:, x * L : (x + 1) * L]

    leave = [
        pltpu.make_async_copy(source, target, sems.at[index])
        for index, (source, target) in enumerate(
            zip(
                (result_ref, grad_feat_ref, total_refs_1[3], total_refs_2[3]),
                (result_out, grad_feat_out, tiles_1_out, tiles_2_out),
            )
        )
    ]

    def flush(ref, copy):
        ref[...] = rows_ref[...].reshape(channels, nx, ny, L).astype(BF)
        copy.start()

    of_coarse.wait()
    coarse_of = moved(5, 1)
    of_skip.wait()
    skip_of = moved(3, 1)

    def result_step(yc, carry):
        for sub in range(2):
            columns = []
            for x in range(nx):
                pieces = []
                for kz in range(3):
                    for ky in range(3):
                        for kx in range(3):
                            pieces.append(coarse_of[kz](yc + (sub + ky + 1) // 2, (x + kx + 1) // 2))
                            pieces.append(skip_of[kz](2 * yc + sub + ky, x + kx))
                columns.append(jnp.concatenate(pieces, axis=0))
            put(2 * yc + sub, dot(w_dec[...], jnp.concatenate(columns, axis=1)))
        return carry

    lax.fori_loop(0, ncy, result_step, 0)
    flush(result_ref, leave[0])
    sum_2.start_exchange()
    of_back.wait()
    back_of = moved(6, 1)
    sum_1.start_gather()

    def feat_step(y, carry):
        put(y, dot(w_enc_t[...], fine(back_of, y)))
        return carry

    lax.fori_loop(0, ny, feat_step, 0)
    sum_2.start_gather()
    flush(grad_feat_ref, leave[1])
    for each in halos:
        each.wait_sent()
    sum_1.finish()
    leave[2].start()
    sum_2.finish()
    leave[3].start()
    for copy in leave:
        copy.wait()


def unpack(
    scale,
    result_in,
    grad_feat_in,
    tiles_1_in,
    tiles_2_in,
    result_out,
    grad_feat_out,
    grad_enc_out,
    grad_down_out,
    grad_dec_out,
    result,
    grad_feat,
    tiles_1,
    tiles_2,
    grad_enc,
    grad_down,
    grad_dec,
    sems,
):
    arrived = [
        pltpu.make_async_copy(source, target, sems.at[index])
        for index, (source, target) in enumerate(zip((tiles_1_in, tiles_2_in, result_in, grad_feat_in), (tiles_1, tiles_2, result, grad_feat)))
    ]
    for copy in arrived:
        copy.start()
    ends = (result_out, grad_feat_out, grad_enc_out, grad_down_out, grad_dec_out)
    leaving = [
        pltpu.make_async_copy(source, target, sems.at[4 + index])
        for index, (source, target) in enumerate(zip((result, grad_feat, grad_enc, grad_down, grad_dec), ends))
    ]
    channels, coarse_channels = grad_down.shape[1:]
    joined_channels = grad_dec.shape[2]
    tiles = channels // 16
    dec_tiles = 27 * tiles
    arrived[0].wait()
    for index, place in enumerate(PLACE):
        held = tiles_1[index * tiles : (index + 1) * tiles].astype(F32).reshape(channels, L)
        grad_dec[26 - place] = held[:, :joined_channels] * scale
    leaving[4].start()
    half = 27 * channels // 2
    both = tiles_1[dec_tiles : dec_tiles + half // 16].astype(F32).reshape(half, L) * scale
    whole = jnp.concatenate([both[:, :coarse_channels], both[:, coarse_channels:]], axis=0)
    for index, place in enumerate(PLACE):
        grad_down[place] = whole[index * channels : (index + 1) * channels]
    leaving[3].start()
    arrived[1].wait()
    across_tiles = pl.cdiv(27 * channels, L)
    for index, place in enumerate(PLACE):
        lane = index * channels
        for h in range(tiles):
            tile = tiles_2[h * across_tiles + lane // L].astype(F32)
            grad_enc[place, 16 * h : 16 * h + 16] = tile[:, lane % L : lane % L + channels] * scale
    leaving[2].start()
    for index in (0, 1):
        arrived[2 + index].wait()
        leaving[index].start()
    for copy in leaving:
        copy.wait()


def shards(sizes, feat, w_enc, w_down, w_dec, cotangent):
    channels, nx, ny, nz = feat.shape
    coarse_channels = w_down.shape[0]
    joined_channels = channels + coarse_channels
    ncy = ny // 2
    count = sizes[1] * sizes[2]
    tiles_1 = 27 * channels // 16 + 27 * channels // 32
    tiles_2 = channels // 16 * pl.cdiv(27 * channels, L)
    owners_1, owners_2 = count, min(count, tiles_2)
    each_1, each_2 = pl.cdiv(tiles_1, owners_1), pl.cdiv(tiles_2, owners_2)

    def taps(weight, order):
        return weight.transpose(2, 3, 4, *order).reshape(27, weight.shape[order[0]], weight.shape[order[1]])

    def vmem(*shape, dtype=BF):
        return pltpu.VMEM(shape, dtype)

    def fine(c):
        return vmem(ny + 2, nx + 2, c, L)

    def small(c):
        return vmem(ncy + 2, 3, c, L)

    c1, c2, cj = channels, coarse_channels, joined_channels
    shaped = [fine(c1), fine(c1), small(c1), fine(c1), small(c2), small(c2), fine(c1)]
    scratch = [vmem(*feat.shape)] * 2
    scratch += [vmem(27, c1, c) for c in (c1, c2, cj)]
    scratch += [vmem(*feat.shape)] * 2
    scratch += [
        vmem(c1 * nx * ny, L, dtype=F32),
        vmem(c1, 27 * c1),
        vmem(c1, 27 * c1),
        vmem(c2, 27 * c1),
        vmem(c1, 27 * c2),
        vmem(c1, 27 * cj),
        vmem(cj, 27 * c1),
    ]
    scratch += [shaped] * 3
    scratch += [[vmem(2, 16, L)] * 7, [vmem(2, 9, 16, L)] * 7]
    scratch += [
        vmem(c1, nx * ny * L, dtype=F32),
        vmem(cj, nx * ny * L, dtype=F32),
        vmem(cj, nx * ny * L),
        vmem(27 * c1, cj, dtype=F32),
        vmem(c1, 27 * c1, dtype=F32),
    ]
    for owners, each in ((owners_1, each_1), (owners_2, each_2)):
        scratch.append(
            [
                vmem(owners * each, 16, L),
                vmem(count - 1, each, 16, L),
                vmem(sizes[0], each, 16, L),
                vmem(owners * each, 16, L),
            ]
        )
    scratch += [
        pltpu.SemaphoreType.DMA((7, len(AROUND))),
        pltpu.SemaphoreType.DMA((7, len(AROUND))),
        pltpu.SemaphoreType.DMA((2, 6)),
        pltpu.SemaphoreType.DMA((5,)),
    ]
    apart = pl.BlockSpec(memory_space=pl.ANY)
    fields = [jax.ShapeDtypeStruct(feat.shape, BF)] * 2
    grads = [jax.ShapeDtypeStruct((27, c1, c), F32) for c in (c1, c2, cj)]
    held_tiles = (owners_1 * each_1, owners_2 * each_2)
    tiles = [jax.ShapeDtypeStruct((size, 16, L), BF) for size in held_tiles]
    held = pl.pallas_call(
        functools.partial(kernel, sizes, ((owners_1, each_1), (owners_2, each_2))),
        out_shape=fields + tiles,
        in_specs=[apart] * 5,
        out_specs=[apart] * 4,
        scratch_shapes=scratch,
        compiler_params=pltpu.CompilerParams(
            collective_id=0, has_side_effects=True, vmem_limit_bytes=56 << 20
        ),
    )(feat, cotangent, taps(w_enc, (0, 1)), taps(w_down, (1, 0)), taps(w_dec, (0, 1)))
    scale = 1.0 / math.sqrt(float(nx * ny * nz * sizes[0] * sizes[1] * sizes[2]))
    result, grad_feat, grad_enc, grad_down, grad_dec = pl.pallas_call(
        functools.partial(unpack, scale),
        out_shape=fields + grads,
        in_specs=[apart] * 4,
        out_specs=[apart] * 5,
        scratch_shapes=[pltpu.VMEM(each.shape, each.dtype) for each in fields + tiles + grads]
        + [pltpu.SemaphoreType.DMA((9,))],
        compiler_params=pltpu.CompilerParams(vmem_limit_bytes=60 << 20),
    )(*held)

    def untaps(value, order):
        return value.reshape(3, 3, 3, *value.shape[1:]).transpose(*order, 0, 1, 2)

    return (
        result,
        grad_feat,
        untaps(grad_enc, (3, 4)),
        untaps(grad_down, (4, 3)),
        untaps(grad_dec, (3, 4)),
    )


def solution(mesh):
    sizes = tuple(mesh.shape[axis] for axis in ("slab", "px", "py"))
    placed = P(None, "px", "py", "slab")
    return jax.shard_map(
        functools.partial(shards, sizes),
        mesh=mesh,
        in_specs=(placed, P(), P(), P(), placed),
        out_specs=(placed, placed, P(), P(), P()),
        check_vma=False,
    )
```

time: 74.9 us -> 59.3 us (0.79)
  Pallas kernels: 67.7 us -> 58.5 us
  local copies, waits for them, and re-layouts: 6.3 us -> 0 us
    pallas_call x1, Pallas kernels: 67.7 us -> 56.2 us  [shards(): pl.pallas_call(functools.partial(kernel, sizes, ((owners_1, each_1), (own...]
    unnamed x11 -> x0, local copies, waits for them, and re-layouts: 6.3 us -> none
    pallas_call x0 -> x1, Pallas kernels: none -> 2.29 us  [shards(): pl.pallas_call(functools.partial(unpack, scale), out_shape=fields + grads...]
where the time goes in v2:
time: 59.3 us; the launch traced here: 59.1 us
  Pallas kernels  58.5 us (99%)
  between operations  0.64 us (1%)
    pallas_call x1, Pallas kernels, shards(): pl.pallas_call(functools.partial(kernel, sizes, ((owners_1, each_1), (own...  56.2 us
    pallas_call x1, Pallas kernels, shards(): pl.pallas_call(functools.partial(unpack, scale), out_shape=fields + grads...  2.29 us

profile of v2, /device:TPU:1, one launch (start us, length us, event | category | flops | bytes accessed | tf_op | source)
XLA Modules:
  0.0 59.1 jit_solution(10897534805276371543)
XLA Ops:
  0.6 56.2 %shard_map.92 = (bf16[32,2,8,128]{3,2,1,0:T(8,128)(2,1)}, bf16[32,2,8,128]{3,2,1,0:T(8,128)(2,1)}, bf16[96,16,128]{2,1,0:T(8,128)(2,1)}, bf16[14,16,128]{2,1,0:T(8,128)(2,1)}) custom-call(bf16[32,2,8,128]{3,2,1,0:T(8,128)(2,1)} %feat_in.1, bf16[32,2,8,128]{3,2,1,0:T(8,128)(2,1)} %cot_in.1, bf16[27,32,32]{2,1,0:T(8,128)(2,1)} %bitcast.18, ...), custom_call_target="tpu_custom_call" | custom-call | tf_op jit(solution)/shard_map/pallas_call | solution.py:677
  56.8 2.3 %shard_map.93 = (bf16[32,2,8,128]{3,2,1,0:T(8,128)(2,1)}, bf16[32,2,8,128]{3,2,1,0:T(8,128)(2,1)}, f32[27,32,32]{2,1,0:T(8,128)}, f32[27,32,64]{2,1,0:T(8,128)}, f32[27,32,96]{2,1,0:T(8,128)}) custom-call(bf16[32,2,8,128]{3,2,1,0:T(8,128)(2,1)} %get-tuple-element.14.result_in, bf16[32,2,8,128]{3,2,1,0:T(8,128)(2,1)} %get-tuple-element.15.grad_feat_in, ...), custom_call_target="tpu_custom_call" | custom-call | tf_op jit(solution)/shard_map/pallas_call | solution.py:688

commit v3 on v2

--- a/solution.py
+++ b/solution.py
@@ -298,6 +298,7 @@
     joined_grad,
     own_joined,
     dec_sum,
+    dec_skip_sum,
     enc_sum,
     total_refs_1,
     total_refs_2,
@@ -415,6 +416,18 @@
         return carry
 
     lax.fori_loop(0, ny, back, 0)
+    dec_skip_sum[...] = jnp.zeros_like(dec_skip_sum)
+
+    def dec_skip_step(y, carry):
+        dec_skip_sum[...] += dot_t(fine(cot_of, y), own_joined[coarse_channels:, span_of(y)])
+        return carry
+
+    lax.fori_loop(0, ny, dec_skip_step, 0)
+    held_rows = 7 * channels
+    quarters = [dec_skip_sum[q * held_rows : (q + 1) * held_rows] for q in range(3)]
+    quarters.append(jnp.concatenate([dec_skip_sum[3 * held_rows :], jnp.zeros((channels, channels), F32)], axis=0))
+    skip_tiles = jnp.concatenate(quarters, axis=1).astype(BF).reshape(held_rows // 16, 16, L)
+    terms_2[terms_2.shape[0] - held_rows // 16 :] = skip_tiles
     of_pool.wait()
     pool_of = moved(2, 2)
     pooled_patch = jnp.concatenate([patch(*pool_of, yc, 0) for yc in range(ncy)], axis=1)
@@ -446,15 +459,14 @@
     dec_sum[...] = jnp.zeros_like(dec_sum)
 
     def dec_step(y, carry):
-        dec_sum[...] += dot_t(fine(cot_of, y), own_joined[:, span_of(y)])
+        dec_sum[...] += dot_t(fine(cot_of, y), own_joined[:coarse_channels, span_of(y)])
         return carry
 
     lax.fori_loop(0, ny, dec_step, 0)
-    dec_tiles = dec_sum.shape[0] // 16
-    down_tiles = half // 16
-    terms_1[0:dec_tiles, :, 0:joined_channels] = dec_sum[...].astype(BF).reshape(dec_tiles, 16, joined_channels)
-    paired = jnp.concatenate([down_sum[:half], down_sum[half:]], axis=1)
-    terms_1[dec_tiles : dec_tiles + down_tiles] = paired.astype(BF).reshape(down_tiles, 16, L)
+    tiles = half // 16
+    for index, value in enumerate((dec_sum[...], down_sum)):
+        paired = jnp.concatenate([value[:half], value[half:]], axis=1)
+        terms_1[index * tiles : (index + 1) * tiles] = paired.astype(BF).reshape(tiles, 16, L)
     sum_1.start_scatter()
     of_slope.wait()
     slope_of = moved(4, 2)
@@ -484,8 +496,6 @@
             terms_2[h * pl.cdiv(wide, L) + at_lane // L, :, 0:size] = piece.astype(BF)
     sum_2.start_scatter()
     of_back.start()
-    sum_1.start_exchange()
-
     def put(y, value):
         for x in range(nx):
             rows_ref[pl.ds(x * ny + y, channels, stride=across), :] = value[:, x * L : (x + 1) * L]
@@ -509,6 +519,7 @@
     of_skip.wait()
     skip_of = moved(3, 1)
 
+    sum_1.start_exchange()
     def result_step(yc, carry):
         for sub in range(2):
             columns = []
@@ -524,12 +535,11 @@
         return carry
 
     lax.fori_loop(0, ncy, result_step, 0)
+    sum_2.start_exchange()
     flush(result_ref, leave[0])
-    sum_2.start_exchange()
+    sum_1.start_gather()
     of_back.wait()
     back_of = moved(6, 1)
-    sum_1.start_gather()
-
     def feat_step(y, carry):
         put(y, dot(w_enc_t[...], fine(back_of, y)))
         return carry
@@ -537,6 +547,7 @@
     lax.fori_loop(0, ny, feat_step, 0)
     sum_2.start_gather()
     flush(grad_feat_ref, leave[1])
+
     for each in halos:
         each.wait_sent()
     sum_1.finish()
@@ -579,21 +590,29 @@
         for index, (source, target) in enumerate(zip((result, grad_feat, grad_enc, grad_down, grad_dec), ends))
     ]
     channels, coarse_channels = grad_down.shape[1:]
-    joined_channels = grad_dec.shape[2]
     tiles = channels // 16
-    dec_tiles = 27 * tiles
+    half = 27 * channels // 2
+
+    def unpaired(index):
+        span = tiles_1[index * (half // 16) : (index + 1) * (half // 16)]
+        both = span.astype(F32).reshape(half, L) * scale
+        return jnp.concatenate([both[:, :coarse_channels], both[:, coarse_channels:]], axis=0)
+
     arrived[0].wait()
-    for index, place in enumerate(PLACE):
-        held = tiles_1[index * tiles : (index + 1) * tiles].astype(F32).reshape(channels, L)
-        grad_dec[26 - place] = held[:, :joined_channels] * scale
-    leaving[4].start()
-    half = 27 * channels // 2
-    both = tiles_1[dec_tiles : dec_tiles + half // 16].astype(F32).reshape(half, L) * scale
-    whole = jnp.concatenate([both[:, :coarse_channels], both[:, coarse_channels:]], axis=0)
+    whole = unpaired(1)
     for index, place in enumerate(PLACE):
         grad_down[place] = whole[index * channels : (index + 1) * channels]
     leaving[3].start()
+    whole = unpaired(0)
     arrived[1].wait()
+    first = tiles_2.shape[0] - 7 * tiles
+    for index, place in enumerate(PLACE):
+        quarter, row = divmod(index, 7)
+        span = tiles_2[first + row * tiles : first + (row + 1) * tiles]
+        skip = span.astype(F32).reshape(channels, L)[:, quarter * channels : (quarter + 1) * channels]
+        rows = whole[index * channels : (index + 1) * channels]
+        grad_dec[26 - place] = jnp.concatenate([rows, skip * scale], axis=1)
+    leaving[4].start()
     across_tiles = pl.cdiv(27 * channels, L)
     for index, place in enumerate(PLACE):
         lane = index * channels
@@ -614,10 +633,10 @@
     joined_channels = channels + coarse_channels
     ncy = ny // 2
     count = sizes[1] * sizes[2]
-    tiles_1 = 27 * channels // 16 + 27 * channels // 32
-    tiles_2 = channels // 16 * pl.cdiv(27 * channels, L)
-    owners_1, owners_2 = count, min(count, tiles_2)
-    each_1, each_2 = pl.cdiv(tiles_1, owners_1), pl.cdiv(tiles_2, owners_2)
+    tiles_1 = 2 * (27 * channels // 32)
+    tiles_2 = channels // 16 * pl.cdiv(27 * channels, L) + 7 * channels // 16
+    each_1, each_2 = pl.cdiv(tiles_1, count), pl.cdiv(tiles_2, count)
+    owners_1, owners_2 = pl.cdiv(tiles_1, each_1), pl.cdiv(tiles_2, each_2)
 
     def taps(weight, order):
         return weight.transpose(2, 3, 4, *order).reshape(27, weight.shape[order[0]], weight.shape[order[1]])
@@ -651,7 +670,8 @@
         vmem(c1, nx * ny * L, dtype=F32),
         vmem(cj, nx * ny * L, dtype=F32),
         vmem(cj, nx * ny * L),
-        vmem(27 * c1, cj, dtype=F32),
+        vmem(27 * c1, c2, dtype=F32),
+        vmem(27 * c1, c1, dtype=F32),
         vmem(c1, 27 * c1, dtype=F32),
     ]
     for owners, each in ((owners_1, each_1), (owners_2, each_2)):

time: 59.3 us -> 57.8 us (0.975)
  Pallas kernels: 58.5 us -> 57 us
    pallas_call x1, Pallas kernels: 56.2 us -> 54.7 us  [shards(): pl.pallas_call(functools.partial(kernel, sizes, ((owners_1, each_1), (own...]
where the time goes in v3:
time: 57.8 us; the launch traced here: 57.7 us
  Pallas kernels  57 us (99%)
  between operations  0.64 us (1%)
    pallas_call x1, Pallas kernels, shards(): pl.pallas_call(functools.partial(kernel, sizes, ((owners_1, each_1), (own...  54.7 us
    pallas_call x1, Pallas kernels, shards(): pl.pallas_call(functools.partial(unpack, scale), out_shape=fields + grads...  2.37 us

profile of v3, /device:TPU:1, one launch (start us, length us, event | category | flops | bytes accessed | tf_op | source)
XLA Modules:
  0.0 57.7 jit_solution(9772118138708778373)
XLA Ops:
  0.6 54.7 %shard_map.92 = (bf16[32,2,8,128]{3,2,1,0:T(8,128)(2,1)}, bf16[32,2,8,128]{3,2,1,0:T(8,128)(2,1)}, bf16[54,16,128]{2,1,0:T(8,128)(2,1)}, bf16[28,16,128]{2,1,0:T(8,128)(2,1)}) custom-call(bf16[32,2,8,128]{3,2,1,0:T(8,128)(2,1)} %feat_in.1, bf16[32,2,8,128]{3,2,1,0:T(8,128)(2,1)} %cot_in.1, bf16[27,32,32]{2,1,0:T(8,128)(2,1)} %bitcast.18, ...), custom_call_target="tpu_custom_call" | custom-call | tf_op jit(solution)/shard_map/pallas_call | solution.py:697
  55.3 2.4 %shard_map.93 = (bf16[32,2,8,128]{3,2,1,0:T(8,128)(2,1)}, bf16[32,2,8,128]{3,2,1,0:T(8,128)(2,1)}, f32[27,32,32]{2,1,0:T(8,128)}, f32[27,32,64]{2,1,0:T(8,128)}, f32[27,32,96]{2,1,0:T(8,128)}) custom-call(bf16[32,2,8,128]{3,2,1,0:T(8,128)(2,1)} %get-tuple-element.14.result_in, bf16[32,2,8,128]{3,2,1,0:T(8,128)(2,1)} %get-tuple-element.15.grad_feat_in, ...), custom_call_target="tpu_custom_call" | custom-call | tf_op jit(solution)/shard_map/pallas_call | solution.py:708

commit v4 on v3

--- a/solution.py
+++ b/solution.py
@@ -94,7 +94,6 @@
         return self.width * ((group * self.ny + cell[0]) * self.nx + cell[1])
 
     def start(self):
-        self.start_where(True)
         width = self.width
         lane = lanes() // width
         last = first = jnp.zeros((16, L), F32)
@@ -109,6 +108,7 @@
         self.sent[0] = last.astype(BF)
         self.sent[1] = first.astype(BF)
         self.start_where(False)
+        self.start_where(True)
 
     def clear(self):
         zero = jnp.zeros(self.field.shape[2:], BF)
@@ -453,7 +453,6 @@
             for x in range(nx):
                 cell = ((2 * yc + sub) * nx + x) * L
                 own_joined[:coarse_channels, cell : cell + L] = own
-    of_coarse.start()
     down_sum = dot_t(pooled_patch, jnp.concatenate(grads, axis=1)) * 0.5
     half = down_sum.shape[0] // 2
     dec_sum[...] = jnp.zeros_like(dec_sum)
@@ -468,6 +467,7 @@
         paired = jnp.concatenate([value[:half], value[half:]], axis=1)
         terms_1[index * tiles : (index + 1) * tiles] = paired.astype(BF).reshape(tiles, 16, L)
     sum_1.start_scatter()
+    of_coarse.start()
     of_slope.wait()
     slope_of = moved(4, 2)
     slope_patch = jnp.concatenate([patch(*slope_of, yc, 0) for yc in range(ncy)], axis=1)

time: 57.8 us -> 57 us (0.986)
  Pallas kernels: 57 us -> 56.2 us
    pallas_call x1, Pallas kernels: 54.7 us -> 53.8 us  [shards(): pl.pallas_call(functools.partial(kernel, sizes, ((owners_1, each_1), (own...]
where the time goes in v4:
time: 57 us; the launch traced here: 56.9 us
  Pallas kernels  56.2 us (99%)
  between operations  0.64 us (1%)
    pallas_call x1, Pallas kernels, shards(): pl.pallas_call(functools.partial(kernel, sizes, ((owners_1, each_1), (own...  53.8 us
    pallas_call x1, Pallas kernels, shards(): pl.pallas_call(functools.partial(unpack, scale), out_shape=fields + grads...  2.37 us

profile of v4, /device:TPU:1, one launch (start us, length us, event | category | flops | bytes accessed | tf_op | source)
XLA Modules:
  0.0 56.9 jit_solution(12584017307466309011)
XLA Ops:
  0.6 53.8 %shard_map.92 = (bf16[32,2,8,128]{3,2,1,0:T(8,128)(2,1)}, bf16[32,2,8,128]{3,2,1,0:T(8,128)(2,1)}, bf16[54,16,128]{2,1,0:T(8,128)(2,1)}, bf16[28,16,128]{2,1,0:T(8,128)(2,1)}) custom-call(bf16[32,2,8,128]{3,2,1,0:T(8,128)(2,1)} %feat_in.1, bf16[32,2,8,128]{3,2,1,0:T(8,128)(2,1)} %cot_in.1, bf16[27,32,32]{2,1,0:T(8,128)(2,1)} %bitcast.18, ...), custom_call_target="tpu_custom_call" | custom-call | tf_op jit(solution)/shard_map/pallas_call | solution.py:697
  54.5 2.4 %shard_map.93 = (bf16[32,2,8,128]{3,2,1,0:T(8,128)(2,1)}, bf16[32,2,8,128]{3,2,1,0:T(8,128)(2,1)}, f32[27,32,32]{2,1,0:T(8,128)}, f32[27,32,64]{2,1,0:T(8,128)}, f32[27,32,96]{2,1,0:T(8,128)}) custom-call(bf16[32,2,8,128]{3,2,1,0:T(8,128)(2,1)} %get-tuple-element.14.result_in, bf16[32,2,8,128]{3,2,1,0:T(8,128)(2,1)} %get-tuple-element.15.grad_feat_in, ...), custom_call_target="tpu_custom_call" | custom-call | tf_op jit(solution)/shard_map/pallas_call | solution.py:708
